TPU v7x, 32 devices: a whole 2x2x4 slice. The times are simulated.
32 devices in a mesh: band: 2 (over y), gx: 4 (over z), gy: 2 (over x), gz: 2 (over core).
Axes of the slice: x: 2, y: 2, z: 4, core: 2. Of those that a mesh axis runs over, the one named last changes fastest.
Arguments:
- csm: bfloat16 [2, 4, 512, 512], P(None, 'band', ('gx', 'gy', 'gz')), parts along dimension 1, may hold values from -6 to 6
- positions: float32 [3, 512], replicated, may hold values from -1 to 1
- mic_order: int32 [512], replicated, may hold values from 0 to 511, each once
- wavenumbers: float32 [4], P('band'), parts along dimension 0, may hold values from 20 to 60
Outputs:
- beam_map: float32 [32, 16, 128], P(('band', 'gx'), ('gy', 'gz')), parts along dimension 0
- source_map: float32 [32, 16, 128], P(('band', 'gx'), ('gy', 'gz')), parts along dimension 0
There are 2 independent parts, one for each index of `band`. A program takes and returns all parts, laid end to end along the dimension named above; an argument that names none is the same for every part. Nothing has to cross between parts.
Inputs may be any that keep to these rules, and one draw needn't show every extreme that they name: mic_order names each microphone once.
All inputs are finite; a program needn't handle non-finite values.
Results may differ from a plain program's by a relative error of at most 0.0055.
Values may be sent and summed in bfloat16 or wider, within the bound.
A program may use at most 64 MiB of HBM per device.

v0:
```python
import functools
import math

import jax
import jax.numpy as jnp
import numpy as np
from jax import lax
from jax.experimental import pallas as pl
from jax.experimental.pallas import tpu as pltpu
from jax.sharding import PartitionSpec as P

NY = 128
CX = 4
CZ = 4
ITERS = 3


highest = lax.Precision.HIGHEST


def coords_plane(index, length):
    return (2.0 * index.astype(jnp.float32) + 1.0) / length - 1.0


def coords_depth(index, length):
    return 2.0 + (index.astype(jnp.float32) + 0.5) / length


def steering(cells, placed, rate, factor):
    diff_x = cells[0][None, :] - placed[0][:, None]
    diff_y = cells[1][None, :] - placed[1][:, None]
    diff_z = cells[2][None, :] - placed[2][:, None]
    dist = jnp.sqrt(diff_x * diff_x + diff_y * diff_y + diff_z * diff_z)
    phase = rate * dist
    return (
        (jnp.cos(phase) * factor).astype(jnp.bfloat16),
        (-jnp.sin(phase) * factor).astype(jnp.bfloat16),
    )


def tables(length):
    counter = jnp.arange(length, dtype=jnp.int32)
    angles = (
        2.0 * math.pi / length * (counter[:, None] * counter[None, :] % length).astype(jnp.float32)
    )
    return (jnp.cos(angles), jnp.sin(angles))


def along_axis(table, values, axis):
    formula = {1: "kj,sjbc->skbc", 2: "kj,sajc->sakc", 3: "kj,sabj->sabk"}
    return jnp.einsum(formula[axis], table, values, precision=highest)


def alternate(real_part, imag_part):
    paired = jnp.stack([real_part, imag_part], 1)
    return paired.reshape((2 * real_part.shape[0],) + real_part.shape[1:])


def transform(stack, axis, sign):
    cosine, sine = tables(stack.shape[axis])
    real_part = stack[0::2]
    imag_part = stack[1::2]
    new_real = along_axis(cosine, real_part, axis) - sign * along_axis(sine, imag_part, axis)
    new_imag = along_axis(cosine, imag_part, axis) + sign * along_axis(sine, real_part, axis)
    return alternate(new_real, new_imag)


def forward(signals):
    cosine, sine = tables(signals.shape[3])
    flat = signals.reshape(-1, signals.shape[3])
    real_part = jnp.dot(flat, cosine, precision=highest).reshape(signals.shape)
    imag_part = -jnp.dot(flat, sine, precision=highest).reshape(signals.shape)
    stack = alternate(real_part, imag_part)
    stack = lax.all_to_all(stack, "gx", split_axis=3, concat_axis=1, tiled=True)
    stack = transform(stack, 1, -1.0)
    stack = lax.all_to_all(stack, ("gy", "gz"), split_axis=1, concat_axis=2, tiled=True)
    stack = transform(stack, 2, -1.0)
    return stack


def inverse(stack, total):
    stack = transform(stack, 2, 1.0)
    stack = lax.all_to_all(stack, ("gy", "gz"), split_axis=2, concat_axis=1, tiled=True)
    stack = transform(stack, 1, 1.0)
    stack = lax.all_to_all(stack, "gx", split_axis=1, concat_axis=3, tiled=True)
    cosine, sine = tables(stack.shape[3])
    values = along_axis(cosine, stack[0::2], 3) - along_axis(sine, stack[1::2], 3)
    return values / total


def parity(first, second, third):
    summed = (first[:, None, None] + second[None, :, None] + third[None, None, :]) % 2
    return 1.0 - 2.0 * summed.astype(jnp.float32)


def on_device(csm, positions, mic_order, wavenumbers):
    size_x = lax.axis_size("gx")
    size_y = lax.axis_size("gy")
    size_z = lax.axis_size("gz")
    slab_index = lax.axis_index("gx")
    outer_index = lax.axis_index("gy")
    core_index = lax.axis_index("gz")
    depth_index = outer_index * size_z + core_index
    mics = csm.shape[3]
    bins = csm.shape[1]
    grid_x = CX * size_x
    grid_z = CZ * size_y * size_z
    factor = 1.0 / math.sqrt(mics)
    placed = jnp.take(positions, mic_order, axis=1)
    centre = jnp.stack(
        [
            coords_plane(jnp.full((1,), grid_x // 2, jnp.int32), grid_x),
            coords_plane(jnp.full((1,), NY // 2, jnp.int32), NY),
            coords_depth(jnp.full((1,), grid_z // 2, jnp.int32), grid_z),
        ]
    )
    centre_rows = []
    for which in range(bins):
        centre_re, centre_im = steering(centre, placed, wavenumbers[which], factor)
        centre_rows.append(jnp.concatenate([centre_re, centre_im], 1).T)
    spectra = lax.all_gather(csm, ("gx", "gy", "gz"), axis=2, tiled=True)
    depth_count = CZ
    depth_start = depth_index * CZ
    y_coords = coords_plane(jnp.arange(NY, dtype=jnp.int32), NY)
    z_coords = coords_depth(depth_start + jnp.arange(depth_count, dtype=jnp.int32), grid_z)
    count = depth_count * NY

    def plane(local):
        x_value = coords_plane(slab_index * CX + local, grid_x)
        cells = jnp.stack(
            [
                jnp.broadcast_to(x_value, (count,)),
                jnp.tile(y_coords, depth_count),
                jnp.repeat(z_coords, NY),
            ]
        )
        beam = jnp.zeros((count,), jnp.float32)
        spread = jnp.zeros((count,), jnp.float32)
        for which in range(bins):
            steer_re, steer_im = steering(cells, placed, wavenumbers[which], factor)
            both = jnp.concatenate([steer_re, steer_im], 1)
            first = jnp.dot(spectra[0, which], both, preferred_element_type=jnp.float32)
            second = jnp.dot(spectra[1, which], steer_im, preferred_element_type=jnp.float32)
            rows_re, rows_im = (steer_re, steer_im)
            rows_re = rows_re.astype(jnp.float32)
            rows_im = rows_im.astype(jnp.float32)
            beam = beam + jnp.sum(
                rows_re * first[:, :count] + rows_im * first[:, count:] - 2.0 * rows_re * second,
                axis=0,
            )
            dots = jnp.dot(centre_rows[which], both, preferred_element_type=jnp.float32)
            real_dot = dots[0, :count] + dots[1, count:]
            imag_dot = dots[1, :count] - dots[0, count:]
            spread = spread + (real_dot * real_dot + imag_dot * imag_dot) / bins
        return (beam, spread)

    beams, spreads = lax.map(plane, jnp.arange(CX, dtype=jnp.int32))
    beam_map = beams.reshape(CX, depth_count, NY)
    psf = spreads.reshape(CX, depth_count, NY)
    psf_sum = lax.psum(jnp.sum(psf), ("gx", "gy", "gz"))
    spectrum = forward(jnp.stack([psf, beam_map]))
    x_share = grid_x // (size_y * size_z)
    y_share = NY // size_x
    signs = parity(
        depth_index * x_share + jnp.arange(x_share, dtype=jnp.int32),
        jnp.arange(grid_z, dtype=jnp.int32),
        slab_index * y_share + jnp.arange(y_share, dtype=jnp.int32),
    )
    psf_real = spectrum[0] * signs / psf_sum
    psf_imag = spectrum[1] * signs / psf_sum
    beam_real = spectrum[2]
    beam_imag = spectrum[3]
    total = float(grid_x * NY * grid_z)
    source = jnp.zeros((CX, CZ, NY), jnp.float32)
    for sweep in range(ITERS):
        if sweep == 0:
            resid_real = -beam_real
            resid_imag = -beam_imag
        else:
            source_hat = forward(source[None])
            resid_real = psf_real * source_hat[0] - psf_imag * source_hat[1] - beam_real
            resid_imag = psf_real * source_hat[1] + psf_imag * source_hat[0] - beam_imag
        grad_real = psf_real * resid_real + psf_imag * resid_imag
        grad_imag = psf_real * resid_imag - psf_imag * resid_real
        image_real = psf_real * grad_real - psf_imag * grad_imag
        image_imag = psf_real * grad_imag + psf_imag * grad_real
        spaces = inverse(jnp.stack([grad_real, grad_imag, image_real, image_imag]), total)
        grad = spaces[0]
        image = spaces[1]
        grad_norm, image_norm = lax.psum(
            (jnp.sum(grad * grad), jnp.sum(image * image)), ("gx", "gy", "gz")
        )
        length = grad_norm / (image_norm + 1e-06)
        source = jnp.maximum(source - length * grad, 0.0)
    return (beam_map, source)


BF = jnp.bfloat16
F32 = jnp.float32


def fit_coeffs():
    theta = (np.cos(np.pi * (np.arange(4000) + 0.5) / 4000) + 1.0) * 0.5 * 0.25
    turns = np.sqrt(theta)
    cos_fit = np.polynomial.chebyshev.Chebyshev.fit(theta, np.cos(2 * np.pi * turns), 5)
    sin_fit = np.polynomial.chebyshev.Chebyshev.fit(theta, np.sin(2 * np.pi * turns) / turns, 4)
    to_power = lambda fit: fit.convert(kind=np.polynomial.Polynomial).coef
    return to_power(cos_fit), to_power(sin_fit)


COS_COEF, SIN_COEF = fit_coeffs()


def horner(values, coefs):
    total = float(coefs[-1]) * values + float(coefs[-2])
    for coef in coefs[-3::-1]:
        total = total * values + float(coef)
    return total


def cos_sin(turns, factor):
    magic = float(1.5 * 2.0**23)
    rest = turns - ((turns + magic) - magic)
    square = rest * rest
    cosine = horner(square, COS_COEF * factor)
    sine = horner(square, SIN_COEF * -factor) * rest
    return cosine.astype(BF), sine.astype(BF)


def split(values):
    high = values.astype(BF)
    return high, (values - high.astype(F32)).astype(BF)


def dot(first, second):
    return jnp.dot(first, second, preferred_element_type=F32)


def grid_tables(slabs, depths):
    grid_x, grid_z = CX * slabs, CZ * depths
    rows = np.arange(grid_x * grid_z)
    device, local = rows // (CX * CZ), rows % (CX * CZ)
    at_x = device // depths * CX + local // CZ
    at_z = device % depths * CZ + local % CZ
    freq_x, freq_z = rows // grid_z, rows % grid_z
    angles = (
        -2.0 * np.pi * (freq_x[:, None] * at_x[None] / grid_x + freq_z[:, None] * at_z[None] / grid_z)
    )
    wide = np.block([[np.cos(angles), -np.sin(angles)], [np.sin(angles), np.cos(angles)]])
    lines = np.arange(NY)
    turn = -2.0 * np.pi * (lines[:, None] * lines[None] % NY) / NY
    ahead = np.concatenate([np.cos(turn), np.sin(turn)], 1)

    def halves(table):
        table = table.astype(np.float32)
        high = table.astype(jnp.bfloat16)
        low = (table - high.astype(np.float32)).astype(jnp.bfloat16)
        return high, low

    wide_high, wide_low = halves(wide)
    forth = np.concatenate([wide_high, wide_low, wide_high], 1)
    back = np.concatenate([wide_high.T, wide_low.T, wide_high.T], 1)
    y_high, y_low = halves(ahead)
    y_forth = np.concatenate([y_high, y_low, y_high], 0)
    y_back = np.concatenate([y_high.T, y_low.T, y_high.T], 0)
    return forth, back, y_forth, y_back


def triple_rows(values):
    high, low = split(values)
    return jnp.concatenate([high, high, low], 0)


def triple_lanes(values):
    high, low = split(values)
    return jnp.concatenate([high, high, low], 1)


def stage_forward(stack, count, forth, y_forth):
    lines = dot(triple_lanes(stack), y_forth[...])
    size = stack.shape[0] // count
    pieces = [
        jnp.concatenate([lines[i * size : (i + 1) * size, :NY], lines[i * size : (i + 1) * size, NY:]], 0)
        for i in range(count)
    ]
    wide = pieces[0] if count == 1 else jnp.concatenate(pieces, 1)
    out = dot(forth[...], triple_rows(wide))
    return out[:size], out[size:]


def stage_inverse(real_part, imag_part, back, y_back):
    size = real_part.shape[0]
    out = dot(back[...], triple_rows(jnp.concatenate([real_part, imag_part], 0)))
    return dot(triple_lanes(jnp.concatenate([out[:size], out[size:]], 1)), y_back[...])


def full_sum(values):
    return jnp.sum(jnp.sum(values, axis=0, keepdims=True), axis=1, keepdims=True)


def deconvolve(psf, beam, grid_z, forth, back, y_forth, y_back):
    size = psf.shape[0]
    total = float(size * NY)
    spec_re, spec_im = stage_forward(jnp.concatenate([psf, beam], 0), 2, forth, y_forth)
    row = lax.broadcasted_iota(jnp.int32, (size, NY), 0)
    lane = lax.broadcasted_iota(jnp.int32, (size, NY), 1)
    odd = (row // grid_z + row % grid_z + lane) % 2
    scale = (1.0 - 2.0 * odd.astype(F32)) / full_sum(psf)
    trans_re, trans_im = spec_re[:, :NY] * scale, spec_im[:, :NY] * scale
    beam_re, beam_im = spec_re[:, NY:], spec_im[:, NY:]
    power = trans_re * trans_re + trans_im * trans_im
    data_re = trans_re * beam_re + trans_im * beam_im
    data_im = trans_re * beam_im - trans_im * beam_re
    source = None
    for sweep in range(ITERS):
        if sweep == 0:
            grad_re, grad_im = -data_re, -data_im
        else:
            hat_re, hat_im = stage_forward(source, 1, forth, y_forth)
            grad_re = power * hat_re - data_re
            grad_im = power * hat_im - data_im
        norm = grad_re * grad_re + grad_im * grad_im
        grad_norm = full_sum(norm) / total
        image_norm = full_sum(power * norm) / total
        step = grad_norm / (image_norm + 1e-06) / total
        move = step * stage_inverse(grad_re, grad_im, back, y_back)
        source = jnp.maximum(-move if sweep == 0 else source - move, 0.0)
    return source


def prepare(order, positions, centre, rates, near_x, near_z, near_y, bins, factor, mids):
    mics = order.shape[1]
    hot = (lax.broadcasted_iota(jnp.int32, (mics, mics), 0) == order[...]).astype(F32).astype(BF)
    high, rest = split(positions[...])
    mid_full = positions[...] - high.astype(F32)
    middle = mid_full.astype(BF)
    low = (mid_full - middle.astype(F32)).astype(BF)
    placed = dot(high, hot) + dot(middle, hot) + dot(low, hot)
    columns = placed.T
    wide = (mics, NY)
    near_x[...] = jnp.broadcast_to(columns[:, 0:1], wide)
    near_z[...] = jnp.broadcast_to(columns[:, 2:3], wide)
    y_value = coords_plane(lax.broadcasted_iota(jnp.int32, wide, 1), NY)
    diff = y_value - jnp.broadcast_to(columns[:, 1:2], wide)
    near_y[...] = diff * diff
    diff_x = centre[0] - placed[0:1]
    diff_y = centre[1] - placed[1:2]
    diff_z = centre[2] - placed[2:3]
    square = diff_x * diff_x + diff_y * diff_y + diff_z * diff_z
    dist = square * lax.rsqrt(square)
    for which in range(bins):
        cosine, sine = cos_sin(dist * rates[which], factor)
        cosine, sine = cosine.astype(F32), sine.astype(F32)
        rows = jnp.concatenate(
            [
                jnp.concatenate([cosine, sine], 1),
                jnp.concatenate([sine, -cosine], 1),
                jnp.zeros((6, 2 * mics), F32),
            ],
            0,
        )
        mids[which] = rows.astype(BF)


def steer_rows(chunk, block, depth_start, slab, grid_x, grid_z, rates, near, store, bins, factor):
    near_x, near_z, near_y = near
    mics = near_x.shape[0]
    size = 64
    rows = pl.ds(pl.multiple_of(block * size, size), size)
    below = pl.ds(pl.multiple_of(mics + block * size, size), size)
    x_value = (2.0 * (slab * CX + chunk // (CZ // 2)).astype(F32) + 1.0) / grid_x - 1.0
    diff_x = x_value - near_x[rows]
    plane = diff_x * diff_x + near_y[rows]
    for half in range(2):
        depth = depth_start + chunk % (CZ // 2) * 2 + half
        z_value = 2.0 + (depth.astype(F32) + 0.5) / grid_z
        diff_z = z_value - near_z[rows]
        square = plane + diff_z * diff_z
        dist = square * lax.rsqrt(square)
        for which in range(bins):
            cosine, sine = cos_sin(dist * rates[which], factor)
            store[chunk, which, rows, half * NY : (half + 1) * NY] = cosine
            store[chunk, which, below, half * NY : (half + 1) * NY] = sine


def psf_chunk(chunk, mids, store, bins):
    spread = jnp.zeros((1, 2 * NY), F32)
    for which in range(bins):
        dots = dot(mids[which], store[chunk, which])
        spread = spread + (dots[0:1] * dots[0:1] + dots[1:2] * dots[1:2]) / bins
    return spread


def beam_chunk(chunk, spectra, store, bins):
    mics = spectra.shape[2]
    beam = jnp.zeros((1, 2 * NY), F32)
    for which in range(bins):
        steer_re = store[chunk, which, :mics]
        steer_im = store[chunk, which, mics:]
        first = dot(spectra[0, which], steer_re) + dot(spectra[1, which], steer_im)
        second = dot(spectra[0, which], steer_im)
        both = steer_re.astype(F32) * first + steer_im.astype(F32) * second
        beam = beam + jnp.sum(both, axis=0, keepdims=True)
    return beam


def put_chunk(ref, chunk, values):
    ref[pl.ds(chunk * 2, 1)] = values[:, :NY]
    ref[pl.ds(chunk * 2 + 1, 1)] = values[:, NY:]


def maps_kernel(sizes, spectra, positions, order, rates_ref, beam_ref, psf_ref, store, near_x, near_z, near_y, mids):
    size_x, size_y, size_z, bins = sizes
    grid_x, grid_z = CX * size_x, CZ * size_y * size_z
    mics = order.shape[1]
    factor = 1.0 / math.sqrt(mics)
    slab = lax.axis_index("gx")
    depth_start = (lax.axis_index("gy") * size_z + lax.axis_index("gz")) * CZ
    rates = [rates_ref[which] * (0.5 / math.pi) for which in range(bins)]
    prepare(order, positions, centre_of(grid_x, grid_z), rates, near_x, near_z, near_y, bins, factor, mids)
    near = (near_x, near_z, near_y)
    blocks = mics // 64

    def steer(i, carry):
        steer_rows(i // blocks, i % blocks, depth_start, slab, grid_x, grid_z, rates, near, store, bins, factor)
        return carry

    chunks = CX * CZ // 2
    lax.fori_loop(0, chunks * blocks, steer, 0)

    def sums(chunk, carry):
        put_chunk(psf_ref, chunk, psf_chunk(chunk, mids, store, bins))
        put_chunk(beam_ref, chunk, beam_chunk(chunk, spectra, store, bins))
        return carry

    lax.fori_loop(0, chunks, sums, 0)


def centre_of(grid_x, grid_z):
    return (
        (2.0 * (grid_x // 2) + 1.0) / grid_x - 1.0,
        (2.0 * (NY // 2) + 1.0) / NY - 1.0,
        2.0 + (grid_z // 2 + 0.5) / grid_z,
    )


def deconvolve_kernel(sizes, maps, forth, back, y_forth, y_back, out, whole):
    size_x, size_y, size_z, bins = sizes
    depths = size_y * size_z
    source = deconvolve(maps[0], maps[1], CZ * depths, forth, back, y_forth, y_back)
    whole[...] = source
    own = lax.axis_index("gx") * depths + lax.axis_index("gy") * size_z + lax.axis_index("gz")
    rows = CX * CZ
    out[...] = whole[pl.ds(pl.multiple_of(own * rows, rows), rows)]


def small_device(csm, positions, mic_order, wavenumbers):
    sizes = (lax.axis_size("gx"), lax.axis_size("gy"), lax.axis_size("gz"), csm.shape[1])
    bins, mics = csm.shape[1], csm.shape[3]
    rows = CX * CZ
    count = sizes[0] * sizes[1] * sizes[2]
    scaled = csm * jnp.array([1.0, -2.0], BF)[:, None, None, None]
    spectra = lax.all_gather(scaled, ("gx", "gy", "gz"), axis=2, tiled=True)
    vmem = pl.BlockSpec(memory_space=pltpu.VMEM)
    params = pltpu.CompilerParams(vmem_limit_bytes=48 * 1024 * 1024)
    padded = jnp.pad(positions, ((0, 5), (0, 0)))
    beam, psf = pl.pallas_call(
        functools.partial(maps_kernel, sizes),
        out_shape=[jax.ShapeDtypeStruct((rows, NY), F32)] * 2,
        in_specs=[vmem, vmem, vmem, pl.BlockSpec(memory_space=pltpu.SMEM)],
        out_specs=[vmem, vmem],
        scratch_shapes=[
            pltpu.VMEM((rows // 2, bins, 2 * mics, 2 * NY), BF),
            pltpu.VMEM((mics, NY), F32),
            pltpu.VMEM((mics, NY), F32),
            pltpu.VMEM((mics, NY), F32),
            pltpu.VMEM((bins, 8, 2 * mics), BF),
        ],
        compiler_params=params,
        name="maps",
    )(spectra, padded, mic_order[None], wavenumbers)
    maps = lax.all_gather(jnp.stack([psf, beam]), ("gx", "gy", "gz"), axis=1, tiled=True)
    tables_of = [jnp.asarray(t) for t in grid_tables(sizes[0], sizes[1] * sizes[2])]
    source = pl.pallas_call(
        functools.partial(deconvolve_kernel, sizes),
        out_shape=jax.ShapeDtypeStruct((rows, NY), F32),
        in_specs=[vmem] * 5,
        out_specs=vmem,
        scratch_shapes=[pltpu.VMEM((count * rows, NY), F32)],
        compiler_params=params,
        name="deconvolve",
    )(maps, *tables_of)
    return beam.reshape(CX, CZ, NY), source.reshape(CX, CZ, NY)


def solution(mesh):
    sizes = mesh.shape
    devices = sizes["gx"] * sizes["gy"] * sizes["gz"]
    body = small_device if devices <= 16 else on_device
    return jax.shard_map(
        body,
        mesh=mesh,
        in_specs=(P(None, "band", ("gx", "gy", "gz"), None), P(), P(), P("band")),
        out_specs=(P(("band", "gx"), ("gy", "gz"), None), P(("band", "gx"), ("gy", "gz"), None)),
        check_vma=False,
    )
```

profile of v0, /device:TPU:0, one launch (start us, length us, event | category | flops | bytes accessed | tf_op | source)
XLA Modules:
  0.0 114.4 jit_solution(5287372278321689817)
XLA Ops:
  7.2 0.0 copy-start.3
  7.2 0.0 copy-start.4
  7.2 0.0 all-gather.2.cloned.1.call-start
  7.2 1.7 %broadcast_multiply_fusion = bf16[2,2,32,512]{3,2,1,0:T(8,128)(2,1)} fusion(bf16[2,2,32,512]{3,2,1,0:T(8,128)(2,1)} %param.9, bf16[2]{0:T(256)(128)(2,1)} %constant.13.clone), kind=kLoop, calls=%fused_computation | loop fusion | flops 65536 | bytes 262148 | tf_op jit(solution)/shard_map/mul | solution.py:462
  9.0 0.0 all-gather.2.cloned.1.call-update
  9.0 0.7 pad.4.positions
  9.7 44.6 %all-gather.2.cloned.1.call-done.spectra = bf16[2,2,512,512]{3,2,1,0:T(8,128)(2,1)} async-done(((bf16[2,2,32,512]{3,2,1,0:T(8,128)(2,1)}), bf16[2,2,512,512]{3,2,1,0:T(8,128)(2,1)}) %all-gather.2.cloned.1.call-update) | async-done | bytes 2097168 | tf_op jit(solution)/shard_map/all_gather | solution.py:463
  54.3 0.0 copy-start
  54.3 1.6 %copy-done = bf16[2,2,512,512]{3,2,1,0:T(8,128)(2,1)S(1)} copy-done((bf16[2,2,512,512]{3,2,1,0:T(8,128)(2,1)S(1)}, bf16[2,2,512,512]{3,2,1,0:T(8,128)(2,1)}, u32[]{:S(2)}) %copy-start) | copy-done | bytes 2097176
  55.9 0.0 copy-start.5
  55.9 0.7 copy-done.5
  56.6 0.0 copy-start.6
  56.6 0.7 copy-done.6
  57.2 0.0 copy-start.1
  57.2 20.8 %maps.1 = (f32[16,128]{1,0:T(8,128)}, f32[16,128]{1,0:T(8,128)S(1)}) custom-call(bf16[2,2,512,512]{3,2,1,0:T(8,128)(2,1)S(1)} %copy-done, f32[8,512]{1,0:T(8,128)S(1)} %pad.4.positions, s32[1,512]{1,0:T(1,128)S(1)} %bitcast.6, f32[2]{0:T(128)S(1)} %copy-done.6), custom_call_target="tpu_custom_call" | custom-call | tf_op jit(solution)/shard_map/maps/pallas_call | solution.py:467
  78.0 0.7 pad_maximum_fusion
  78.7 19.9 %all_gather.7.maps = f32[2,256,128]{2,1,0:T(8,128)S(1)} all-gather(f32[2,16,128]{2,1,0:T(8,128)S(1)} %pad_maximum_fusion), channel_id=1, replica_groups=mesh['band'=2,'gx'=4,'gy'=2,'gz'=2] {'gx','gy','gz'}, dimensions={1}, use_global_device_ids=true | all-gather | bytes 278528 | tf_op jit(solution)/shard_map/all_gather | solution.py:482
  98.6 0.0 copy-done.3
  98.6 0.0 copy-done.4
  98.6 0.0 copy-done.1
  98.6 0.0 copy-start.2
  98.6 1.4 %copy-done.2 = bf16[512,1536]{1,0:T(8,128)(2,1)S(1)} copy-done((bf16[512,1536]{1,0:T(8,128)(2,1)S(1)}, bf16[512,1536]{1,0:T(8,128)(2,1)}, u32[]{:S(2)}) %copy-start.2) | copy-done | bytes 1572888
  100.0 7.5 %deconvolve.1 = f32[16,128]{1,0:T(8,128)} custom-call(f32[2,256,128]{2,1,0:T(8,128)S(1)} %all_gather.7.maps, bf16[512,1536]{1,0:T(8,128)(2,1)S(1)} %copy-done.1, bf16[512,1536]{1,0:T(8,128)(2,1)S(1)} %copy-done.2, bf16[384,256]{1,0:T(8,128)(2,1)S(1)} %copy-done.3, bf16[768,128]{1,0:T(8,128)(2,1)S(1)} %copy-done.4), custom_call_target="tpu_custom_call" | custom-call | tf_op jit(solution)/shard_map/deconvolve/pallas_call | solution.py:484
Async XLA Ops:
  7.2 91.4 %copy-start.3 = (bf16[384,256]{1,0:T(8,128)(2,1)S(1)}, bf16[384,256]{1,0:T(8,128)(2,1)}, u32[]{:S(2)}) copy-start(bf16[384,256]{1,0:T(8,128)(2,1)} %constant.16.clone.y_forth) | copy-start | bytes 589828
  7.2 91.4 %copy-start.4 = (bf16[768,128]{1,0:T(8,128)(2,1)S(1)}, bf16[768,128]{1,0:T(8,128)(2,1)}, u32[]{:S(2)}) copy-start(bf16[768,128]{1,0:T(8,128)(2,1)} %constant.17.clone.y_back) | copy-start | bytes 589828
  7.2 47.1 %all-gather.2.cloned.1.call-start = ((), (), s32[]{:S(2)}) async-start(), calls=%async_computation | async-start | bytes 2228224 | tf_op jit(solution)/shard_map/all_gather | solution.py:463
  54.3 1.6 %copy-start = (bf16[2,2,512,512]{3,2,1,0:T(8,128)(2,1)S(1)}, bf16[2,2,512,512]{3,2,1,0:T(8,128)(2,1)}, u32[]{:S(2)}) copy-start(bf16[2,2,512,512]{3,2,1,0:T(8,128)(2,1)} %all-gather.2.cloned.1.call-done.spectra) | copy-start | bytes 6291460
  55.9 0.7 copy-start.5
  56.6 0.7 copy-start.6
  57.2 41.4 %copy-start.1 = (bf16[512,1536]{1,0:T(8,128)(2,1)S(1)}, bf16[512,1536]{1,0:T(8,128)(2,1)}, u32[]{:S(2)}) copy-start(bf16[512,1536]{1,0:T(8,128)(2,1)} %constant.14.clone.forth) | copy-start | bytes 4718596
  98.6 1.4 %copy-start.2 = (bf16[512,1536]{1,0:T(8,128)(2,1)S(1)}, bf16[512,1536]{1,0:T(8,128)(2,1)}, u32[]{:S(2)}) copy-start(bf16[512,1536]{1,0:T(8,128)(2,1)} %constant.15.clone.back) | copy-start | bytes 4718596
Sparse Core Ops, SparseCore 0:
  10.2 44.0 all-gather.1
where the time goes:
time: 115 us; the launch traced here: 114 us
  waiting for transfers between devices  44.6 us (39%)
  Pallas kernels  28.3 us (25%)
  blocking collectives  19.9 us (17%)
  between operations  14.1 us (12%)
  local copies, waits for them, and re-layouts  5.05 us (4%)
  other arithmetic  2.44 us (2%)
    all_gather x1, waiting for transfers between devices, small_device(): spectra = lax.all_gather(scaled, ('gx', 'gy', 'gz'), axis=2, tiled=True)  44.6 us
    pallas_call x1, Pallas kernels, small_device(): pl.pallas_call(functools.partial(maps_kernel, sizes), out_shape=[jax.Shap...  20.8 us
    all_gather x1, blocking collectives, small_device(): lax.all_gather(jnp.stack([psf, beam]), ('gx', 'gy', 'gz'), axis=1, tiled=...  19.9 us
    pallas_call x1, Pallas kernels, small_device(): pl.pallas_call(functools.partial(deconvolve_kernel, sizes), out_shape=jax...  7.51 us
    unnamed x14, local copies, waits for them, and re-layouts  4.35 us
  transfers between devices with their start and end apart: 1, of which 1 were waited for; matrix products, arithmetic and copies ran while one was open for 1% of the time, Pallas kernels for 0%

commit v1 on v0

--- a/solution.py
+++ b/solution.py
@@ -298,16 +298,20 @@
     return jnp.sum(jnp.sum(values, axis=0, keepdims=True), axis=1, keepdims=True)
 
 
-def deconvolve(psf, beam, grid_z, forth, back, y_forth, y_back):
-    size = psf.shape[0]
-    total = float(size * NY)
-    spec_re, spec_im = stage_forward(jnp.concatenate([psf, beam], 0), 2, forth, y_forth)
-    row = lax.broadcasted_iota(jnp.int32, (size, NY), 0)
-    lane = lax.broadcasted_iota(jnp.int32, (size, NY), 1)
+def transfer_of(psf, grid_z, forth, y_forth):
+    spec_re, spec_im = stage_forward(psf, 1, forth, y_forth)
+    shape = psf.shape
+    row = lax.broadcasted_iota(jnp.int32, shape, 0)
+    lane = lax.broadcasted_iota(jnp.int32, shape, 1)
     odd = (row // grid_z + row % grid_z + lane) % 2
     scale = (1.0 - 2.0 * odd.astype(F32)) / full_sum(psf)
-    trans_re, trans_im = spec_re[:, :NY] * scale, spec_im[:, :NY] * scale
-    beam_re, beam_im = spec_re[:, NY:], spec_im[:, NY:]
+    return spec_re * scale, spec_im * scale
+
+
+def deconvolve(transfer, beam, forth, back, y_forth, y_back):
+    total = float(beam.shape[0] * NY)
+    trans_re, trans_im = transfer
+    beam_re, beam_im = stage_forward(beam, 1, forth, y_forth)
     power = trans_re * trans_re + trans_im * trans_im
     data_re = trans_re * beam_re + trans_im * beam_im
     data_im = trans_re * beam_im - trans_im * beam_re
@@ -331,8 +335,9 @@
 def prepare(order, positions, centre, rates, near_x, near_z, near_y, bins, factor, mids):
     mics = order.shape[1]
     hot = (lax.broadcasted_iota(jnp.int32, (mics, mics), 0) == order[...]).astype(F32).astype(BF)
-    high, rest = split(positions[...])
-    mid_full = positions[...] - high.astype(F32)
+    values = jnp.concatenate([positions[...], jnp.zeros((5, mics), F32)], 0)
+    high = values.astype(BF)
+    mid_full = values - high.astype(F32)
     middle = mid_full.astype(BF)
     low = (mid_full - middle.astype(F32)).astype(BF)
     placed = dot(high, hot) + dot(middle, hot) + dot(low, hot)
@@ -405,35 +410,12 @@
 
 
 def put_chunk(ref, chunk, values):
-    ref[pl.ds(chunk * 2, 1)] = values[:, :NY]
-    ref[pl.ds(chunk * 2 + 1, 1)] = values[:, NY:]
-
-
-def maps_kernel(sizes, spectra, positions, order, rates_ref, beam_ref, psf_ref, store, near_x, near_z, near_y, mids):
-    size_x, size_y, size_z, bins = sizes
-    grid_x, grid_z = CX * size_x, CZ * size_y * size_z
-    mics = order.shape[1]
-    factor = 1.0 / math.sqrt(mics)
-    slab = lax.axis_index("gx")
-    depth_start = (lax.axis_index("gy") * size_z + lax.axis_index("gz")) * CZ
-    rates = [rates_ref[which] * (0.5 / math.pi) for which in range(bins)]
-    prepare(order, positions, centre_of(grid_x, grid_z), rates, near_x, near_z, near_y, bins, factor, mids)
-    near = (near_x, near_z, near_y)
-    blocks = mics // 64
-
-    def steer(i, carry):
-        steer_rows(i // blocks, i % blocks, depth_start, slab, grid_x, grid_z, rates, near, store, bins, factor)
-        return carry
-
-    chunks = CX * CZ // 2
-    lax.fori_loop(0, chunks * blocks, steer, 0)
-
-    def sums(chunk, carry):
-        put_chunk(psf_ref, chunk, psf_chunk(chunk, mids, store, bins))
-        put_chunk(beam_ref, chunk, beam_chunk(chunk, spectra, store, bins))
-        return carry
-
-    lax.fori_loop(0, chunks, sums, 0)
+    ref[chunk // 2, pl.ds(chunk % 2 * 2, 1)] = values[:, :NY]
+    ref[chunk // 2, pl.ds(chunk % 2 * 2 + 1, 1)] = values[:, NY:]
+
+
+RIGHT, LEFT, ACROSS, SIBLING = range(4)
+MESH = pl.DeviceIdType.MESH
 
 
 def centre_of(grid_x, grid_z):
@@ -444,61 +426,283 @@
     )
 
 
-def deconvolve_kernel(sizes, maps, forth, back, y_forth, y_back, out, whole):
+def whole_kernel(
+    sizes,
+    csm,
+    positions,
+    order,
+    rates_ref,
+    forth_in,
+    back_in,
+    y_forth_in,
+    y_back_in,
+    beam_ref,
+    source_ref,
+    spectra,
+    store,
+    near_x,
+    near_z,
+    near_y,
+    mids,
+    maps,
+    own_psf,
+    forth,
+    back,
+    y_forth,
+    y_back,
+    result,
+    table_sem,
+    block_sent,
+    block_got,
+    map_sent,
+    map_got,
+):
     size_x, size_y, size_z, bins = sizes
-    depths = size_y * size_z
-    source = deconvolve(maps[0], maps[1], CZ * depths, forth, back, y_forth, y_back)
-    whole[...] = source
-    own = lax.axis_index("gx") * depths + lax.axis_index("gy") * size_z + lax.axis_index("gz")
+    grid_x, grid_z = CX * size_x, CZ * size_y * size_z
+    mics = order.shape[1]
+    share = csm.shape[2]
+    devices = size_x * size_y * size_z
+    factor = 1.0 / math.sqrt(mics)
+    at_x, at_y, at_z = lax.axis_index("gx"), lax.axis_index("gy"), lax.axis_index("gz")
+
+    def number(x, y, z):
+        return (x * size_y + y) * size_z + z
+
+    own = number(at_x, at_y, at_z)
+    depth_start = (at_y * size_z + at_z) * CZ
+
+    def place(device):
+        return {
+            "gx": device // (size_y * size_z),
+            "gy": device // size_z % size_y,
+            "gz": device % size_z,
+        }
+
+    barrier = pltpu.get_barrier_semaphore()
+
+    def greet(i, carry):
+        pl.semaphore_signal(
+            barrier, inc=1, device_id=place((own + i) % devices), device_id_type=MESH
+        )
+        return carry
+
+    lax.fori_loop(1, devices, greet, 0)
+    loads = [
+        pltpu.make_async_copy(source, target, table_sem.at[i])
+        for i, (source, target) in enumerate(
+            [(forth_in, forth), (back_in, back), (y_forth_in, y_forth), (y_back_in, y_back)]
+        )
+    ]
+    for load in loads:
+        load.start()
+
+    def rows_of(block):
+        return pl.ds(pl.multiple_of(block * share, share), share)
+
+    spectra[0, :, rows_of(own)] = csm[0]
+    spectra[1, :, rows_of(own)] = (csm[1].astype(F32) * -2.0).astype(BF)
+    pl.semaphore_wait(barrier, devices - 1)
+
+    sends = []
+
+    def block_copy(block, way, target):
+        view = spectra.at[:, :, rows_of(block)]
+        return pltpu.make_async_remote_copy(
+            src_ref=view,
+            dst_ref=view,
+            send_sem=block_sent.at[way, block],
+            recv_sem=block_got.at[block],
+            device_id=target,
+            device_id_type=MESH,
+        )
+
+    sibling, across = {"gz": 1 - at_z}, {"gy": 1 - at_y}
+
+    def along(sign):
+        return {"gx": at_x + sign}
+
+    def send(valid, block, way, target):
+        sends.append((valid, block, way, target))
+
+        @pl.when(valid)
+        def _():
+            block_copy(block, way, target).start()
+
+    def await_block(valid, block):
+        @pl.when(valid)
+        def _():
+            block_copy(block, SIBLING, sibling).wait_recv()
+
+    def inside(x):
+        return (x >= 0) & (x < size_x)
+
+    always = at_x >= 0
+
+    for sign, way in ((1, RIGHT), (-1, LEFT)):
+        send(inside(at_x + sign), own, way, along(sign))
+    send(always, own, ACROSS, across)
+    send(always, own, SIBLING, sibling)
+
+    def pass_on(distance):
+        for sign, way in ((1, RIGHT), (-1, LEFT)):
+            source = at_x - sign * distance
+            block = number(source, at_y, at_z)
+            valid = inside(source)
+            await_block(valid, block)
+            if distance < size_x - 1:
+                send(valid & inside(at_x + sign), block, way, along(sign))
+            send(valid, block, ACROSS, across)
+            send(valid, block, SIBLING, sibling)
+
+    def pass_across(distance):
+        for sign in (1, -1) if distance else (1,):
+            source = at_x - sign * distance
+            block = number(source, 1 - at_y, at_z)
+            valid = inside(source)
+            await_block(valid, block)
+            send(valid, block, SIBLING, sibling)
+
+    rates = [rates_ref[which] * (0.5 / math.pi) for which in range(bins)]
+    prepare(
+        order, positions, centre_of(grid_x, grid_z), rates, near_x, near_z, near_y, bins, factor, mids
+    )
+    near = (near_x, near_z, near_y)
+    blocks = mics // 64
+
+    def steer(i, carry):
+        steer_rows(
+            i // blocks, i % blocks, depth_start, at_x, grid_x, grid_z, rates, near, store, bins, factor
+        )
+        return carry
+
+    chunks = CX * CZ // 2
+    part = chunks * blocks // 4
+    for stage in range(4):
+        lax.fori_loop(part * stage, part * (stage + 1), steer, 0)
+        if stage < 3 and stage + 1 < size_x:
+            pass_on(stage + 1)
+        if 0 < stage < 3 and stage - 1 < size_x:
+            pass_across(stage - 1)
+
     rows = CX * CZ
-    out[...] = whole[pl.ds(pl.multiple_of(own * rows, rows), rows)]
+
+    def psf_step(chunk, carry):
+        put_chunk(own_psf, chunk, psf_chunk(chunk, mids, store, bins))
+        return carry
+
+    lax.fori_loop(0, chunks, psf_step, 0)
+
+    def map_rows(device):
+        return pl.ds(pl.multiple_of(device * rows, rows), rows)
+
+    def map_copy(which, i, source):
+        target = (own + i) % devices
+        return pltpu.make_async_remote_copy(
+            src_ref=maps.at[which, map_rows(source)],
+            dst_ref=maps.at[which, map_rows(source)],
+            send_sem=map_sent.at[which, i],
+            recv_sem=map_got.at[which, source],
+            device_id=place(target),
+            device_id_type=MESH,
+        )
+
+    def spread_map(which, values):
+        maps[which, map_rows(own)] = jnp.concatenate([values[x] for x in range(CX)], 0)
+
+        def start(i, carry):
+            map_copy(which, i, own).start()
+            return carry
+
+        lax.fori_loop(1, devices, start, 0)
+
+    def await_map(which):
+        def one(i, carry):
+            map_copy(which, i, (own + i) % devices).wait_recv()
+            return carry
+
+        lax.fori_loop(1, devices, one, 0)
+
+    spread_map(0, own_psf[...])
+    for distance in range(2, size_x):
+        pass_across(distance)
+    for x in range(size_x):
+        for y in range(size_y):
+            await_block(always, number(x, y, 1 - at_z))
+
+    def beam_step(chunk, carry):
+        put_chunk(beam_ref, chunk, beam_chunk(chunk, spectra, store, bins))
+        return carry
+
+    lax.fori_loop(0, chunks, beam_step, 0)
+    spread_map(1, beam_ref[...])
+    for load in loads:
+        load.wait()
+    await_map(0)
+    transfer = transfer_of(maps[0], grid_z, forth, y_forth)
+    await_map(1)
+    result[...] = deconvolve(transfer, maps[1], forth, back, y_forth, y_back)
+    for x in range(CX):
+        source_ref[x] = result[pl.ds(pl.multiple_of(own * rows, rows) + x * CZ, CZ)]
+
+    for valid, block, way, target in sends:
+
+        @pl.when(valid)
+        def _():
+            block_copy(block, way, target).wait_send()
+
+    def sent(i, carry):
+        for which in range(2):
+            map_copy(which, i, own).wait_send()
+        return carry
+
+    lax.fori_loop(1, devices, sent, 0)
 
 
 def small_device(csm, positions, mic_order, wavenumbers):
     sizes = (lax.axis_size("gx"), lax.axis_size("gy"), lax.axis_size("gz"), csm.shape[1])
     bins, mics = csm.shape[1], csm.shape[3]
     rows = CX * CZ
-    count = sizes[0] * sizes[1] * sizes[2]
-    scaled = csm * jnp.array([1.0, -2.0], BF)[:, None, None, None]
-    spectra = lax.all_gather(scaled, ("gx", "gy", "gz"), axis=2, tiled=True)
+    devices = sizes[0] * sizes[1] * sizes[2]
     vmem = pl.BlockSpec(memory_space=pltpu.VMEM)
-    params = pltpu.CompilerParams(vmem_limit_bytes=48 * 1024 * 1024)
-    padded = jnp.pad(positions, ((0, 5), (0, 0)))
-    beam, psf = pl.pallas_call(
-        functools.partial(maps_kernel, sizes),
-        out_shape=[jax.ShapeDtypeStruct((rows, NY), F32)] * 2,
-        in_specs=[vmem, vmem, vmem, pl.BlockSpec(memory_space=pltpu.SMEM)],
+    anywhere = pl.BlockSpec(memory_space=pl.ANY)
+    tables_of = [jnp.asarray(t) for t in grid_tables(sizes[0], sizes[1] * sizes[2])]
+    beam, source = pl.pallas_call(
+        functools.partial(whole_kernel, sizes),
+        out_shape=[jax.ShapeDtypeStruct((CX, CZ, NY), F32)] * 2,
+        in_specs=[vmem, vmem, vmem, pl.BlockSpec(memory_space=pltpu.SMEM)] + [anywhere] * 4,
         out_specs=[vmem, vmem],
         scratch_shapes=[
+            pltpu.VMEM((2, bins, mics, mics), BF),
             pltpu.VMEM((rows // 2, bins, 2 * mics, 2 * NY), BF),
             pltpu.VMEM((mics, NY), F32),
             pltpu.VMEM((mics, NY), F32),
             pltpu.VMEM((mics, NY), F32),
             pltpu.VMEM((bins, 8, 2 * mics), BF),
+            pltpu.VMEM((2, devices * rows, NY), F32),
+            pltpu.VMEM((CX, CZ, NY), F32),
+        ]
+        + [pltpu.VMEM(t.shape, BF) for t in tables_of]
+        + [
+            pltpu.VMEM((devices * rows, NY), F32),
+            pltpu.SemaphoreType.DMA((4,)),
+            pltpu.SemaphoreType.DMA((4, devices)),
+            pltpu.SemaphoreType.DMA((devices,)),
+            pltpu.SemaphoreType.DMA((2, devices)),
+            pltpu.SemaphoreType.DMA((2, devices)),
         ],
-        compiler_params=params,
-        name="maps",
-    )(spectra, padded, mic_order[None], wavenumbers)
-    maps = lax.all_gather(jnp.stack([psf, beam]), ("gx", "gy", "gz"), axis=1, tiled=True)
-    tables_of = [jnp.asarray(t) for t in grid_tables(sizes[0], sizes[1] * sizes[2])]
-    source = pl.pallas_call(
-        functools.partial(deconvolve_kernel, sizes),
-        out_shape=jax.ShapeDtypeStruct((rows, NY), F32),
-        in_specs=[vmem] * 5,
-        out_specs=vmem,
-        scratch_shapes=[pltpu.VMEM((count * rows, NY), F32)],
-        compiler_params=params,
-        name="deconvolve",
-    )(maps, *tables_of)
-    return beam.reshape(CX, CZ, NY), source.reshape(CX, CZ, NY)
+        compiler_params=pltpu.CompilerParams(
+            vmem_limit_bytes=48 * 1024 * 1024, collective_id=0, has_side_effects=True
+        ),
+        name="maps_and_sources",
+    )(csm, positions, mic_order[None], wavenumbers, *tables_of)
+    return beam, source
 
 
 def solution(mesh):
     sizes = mesh.shape
-    devices = sizes["gx"] * sizes["gy"] * sizes["gz"]
-    body = small_device if devices <= 16 else on_device
+    small = sizes["gx"] <= 4 and sizes["gy"] == 2 and sizes["gz"] == 2
     return jax.shard_map(
-        body,
+        small_device if small else on_device,
         mesh=mesh,
         in_specs=(P(None, "band", ("gx", "gy", "gz"), None), P(), P(), P("band")),
         out_specs=(P(("band", "gx"), ("gy", "gz"), None), P(("band", "gx"), ("gy", "gz"), None)),

time: 115 us -> 55.5 us (0.48)
  waiting for transfers between devices: 44.6 us -> 0 us
  blocking collectives: 19.9 us -> 0 us
  Pallas kernels: 28.3 us -> 45.7 us
  between operations: 14.1 us -> 0.65 us
  local copies, waits for them, and re-layouts: 5.05 us -> 8.8 us
  other arithmetic: 2.44 us -> 0 us
    all_gather x1 -> x0, waiting for transfers between devices: 44.6 us -> none  [small_device(): spectra = lax.all_gather(scaled, ('gx', 'gy', 'gz'), axis=2, tiled=True)]
    all_gather x1 -> x0, blocking collectives: 19.9 us -> none  [small_device(): lax.all_gather(jnp.stack([psf, beam]), ('gx', 'gy', 'gz'), axis=1, tiled=...]
    pallas_call x2 -> x1, Pallas kernels: 28.3 us -> 45.7 us  [small_device(): pl.pallas_call(functools.partial(whole_kernel, sizes), out_shape=[jax.Sha...]
    unnamed x14 -> x18, local copies, waits for them, and re-layouts: 4.35 us -> 8.8 us
    mul x1 -> x0, other arithmetic: 1.74 us -> none  [small_device(): scaled = csm * jnp.array([1.0, -2.0], BF)[:, None, None, None]]
  transfers between devices with their start and end apart: 1 -> 0, of which waited for: 1 -> 0; matrix products, arithmetic and copies ran while one was open for 1% -> 0% of each run, Pallas kernels for 0% -> 0%
where the time goes in v1:
time: 55.5 us; the launch traced here: 55.1 us
  Pallas kernels  45.7 us (82%)
  local copies, waits for them, and re-layouts  8.8 us (16%)
  between operations  0.65 us (1%)
    pallas_call x1, Pallas kernels, small_device(): pl.pallas_call(functools.partial(whole_kernel, sizes), out_shape=[jax.Sha...  45.7 us
    unnamed x18, local copies, waits for them, and re-layouts  8.8 us

profile of v1, /device:TPU:0, one launch (start us, length us, event | category | flops | bytes accessed | tf_op | source)
XLA Modules:
  0.0 55.1 jit_solution(16646000244378955180)
XLA Ops:
  0.6 0.0 copy-start
  0.6 1.4 %copy-done = bf16[512,1536]{1,0:T(8,128)(2,1)S(1)} copy-done((bf16[512,1536]{1,0:T(8,128)(2,1)S(1)}, bf16[512,1536]{1,0:T(8,128)(2,1)}, u32[]{:S(2)}) %copy-start) | copy-done | bytes 1572888
  2.0 0.0 copy-start.1
  2.0 1.4 %copy-done.1 = bf16[512,1536]{1,0:T(8,128)(2,1)S(1)} copy-done((bf16[512,1536]{1,0:T(8,128)(2,1)S(1)}, bf16[512,1536]{1,0:T(8,128)(2,1)}, u32[]{:S(2)}) %copy-start.1) | copy-done | bytes 1572888
  3.5 0.0 copy-start.2
  3.5 0.9 %copy-done.2 = bf16[768,128]{1,0:T(8,128)(2,1)S(1)} copy-done((bf16[768,128]{1,0:T(8,128)(2,1)S(1)}, bf16[768,128]{1,0:T(8,128)(2,1)}, u32[]{:S(2)}) %copy-start.2) | copy-done | bytes 196632
  4.4 0.0 copy-start.3
  4.4 0.9 %copy-done.3 = bf16[384,256]{1,0:T(8,128)(2,1)S(1)} copy-done((bf16[384,256]{1,0:T(8,128)(2,1)S(1)}, bf16[384,256]{1,0:T(8,128)(2,1)}, u32[]{:S(2)}) %copy-start.3) | copy-done | bytes 196632
  5.3 0.0 copy-start.4
  5.3 0.9 %copy-done.4 = bf16[2,2,32,512]{3,2,1,0:T(8,128)(2,1)S(1)} copy-done((bf16[2,2,32,512]{3,2,1,0:T(8,128)(2,1)S(1)}, bf16[2,2,32,512]{3,2,1,0:T(8,128)(2,1)}, u32[]{:S(2)}) %copy-start.4) | copy-done | bytes 131096
  6.2 0.0 copy-start.5
  6.2 0.7 %copy-done.5 = f32[3,512]{1,0:T(4,128)S(1)} copy-done((f32[3,512]{1,0:T(4,128)S(1)}, f32[3,512]{1,0:T(4,128)}, u32[]{:S(2)}) %copy-start.5) | copy-done | bytes 6168
  6.9 0.0 copy-start.6
  6.9 0.7 %copy-done.6 = s32[512]{0:T(512)S(1)} copy-done((s32[512]{0:T(512)S(1)}, s32[512]{0:T(512)}, u32[]{:S(2)}) %copy-start.6) | copy-done | bytes 2072
  7.6 0.0 copy-start.7
  7.6 0.7 %copy-done.7 = f32[2]{0:T(128)S(1)} copy-done((f32[2]{0:T(128)S(1)}, f32[2]{0:T(128)}, u32[]{:S(2)}) %copy-start.7) | copy-done | bytes 32
  8.2 45.7 %maps_and_sources.1 = (f32[4,4,128]{2,1,0:T(4,128)S(1)}, f32[4,4,128]{2,1,0:T(4,128)S(1)}) custom-call(bf16[2,2,32,512]{3,2,1,0:T(8,128)(2,1)S(1)} %copy-done.4, f32[3,512]{1,0:T(4,128)S(1)} %copy-done.5, s32[1,512]{1,0:T(1,128)S(1)} %bitcast.1, f32[2]{0:T(128)S(1)} %copy-done.7, bf16[512,1536]{1,0:T(8,128)(2,1)S(1)} %copy-done.1, ...), custom_call_target="tpu_custom_call" | custom-call | tf_op jit(solution)/shard_map/maps_and_sources/pallas_call | solution.py:669
  53.9 0.6 %copy.12 = f32[4,4,128]{2,1,0:T(4,128)} copy(f32[4,4,128]{2,1,0:T(4,128)S(1)} %get-tuple-element.4) | data formatting | bytes 16384
  54.5 0.6 %copy.13 = f32[4,4,128]{2,1,0:T(4,128)} copy(f32[4,4,128]{2,1,0:T(4,128)S(1)} %get-tuple-element.5) | data formatting | bytes 16384
Async XLA Ops:
  0.6 1.4 %copy-start = (bf16[512,1536]{1,0:T(8,128)(2,1)S(1)}, bf16[512,1536]{1,0:T(8,128)(2,1)}, u32[]{:S(2)}) copy-start(bf16[512,1536]{1,0:T(8,128)(2,1)} %constant.9.clone.back_in) | copy-start | bytes 4718596
  2.0 1.4 %copy-start.1 = (bf16[512,1536]{1,0:T(8,128)(2,1)S(1)}, bf16[512,1536]{1,0:T(8,128)(2,1)}, u32[]{:S(2)}) copy-start(bf16[512,1536]{1,0:T(8,128)(2,1)} %constant.8.clone.forth_in) | copy-start | bytes 4718596
  3.5 0.9 %copy-start.2 = (bf16[768,128]{1,0:T(8,128)(2,1)S(1)}, bf16[768,128]{1,0:T(8,128)(2,1)}, u32[]{:S(2)}) copy-start(bf16[768,128]{1,0:T(8,128)(2,1)} %constant.11.clone.y_back_in) | copy-start | bytes 589828
  4.4 0.9 %copy-start.3 = (bf16[384,256]{1,0:T(8,128)(2,1)S(1)}, bf16[384,256]{1,0:T(8,128)(2,1)}, u32[]{:S(2)}) copy-start(bf16[384,256]{1,0:T(8,128)(2,1)} %constant.10.clone.y_forth_in) | copy-start | bytes 589828
  5.3 0.9 %copy-start.4 = (bf16[2,2,32,512]{3,2,1,0:T(8,128)(2,1)S(1)}, bf16[2,2,32,512]{3,2,1,0:T(8,128)(2,1)}, u32[]{:S(2)}) copy-start(bf16[2,2,32,512]{3,2,1,0:T(8,128)(2,1)} %csm.1) | copy-start | bytes 393220
  6.2 0.7 %copy-start.5 = (f32[3,512]{1,0:T(4,128)S(1)}, f32[3,512]{1,0:T(4,128)}, u32[]{:S(2)}) copy-start(f32[3,512]{1,0:T(4,128)} %positions.1) | copy-start | bytes 18436
  6.9 0.7 %copy-start.6 = (s32[512]{0:T(512)S(1)}, s32[512]{0:T(512)}, u32[]{:S(2)}) copy-start(s32[512]{0:T(512)} %param.10) | copy-start | bytes 6148
  7.6 0.7 %copy-start.7 = (f32[2]{0:T(128)S(1)}, f32[2]{0:T(128)}, u32[]{:S(2)}) copy-start(f32[2]{0:T(128)} %rates_ref.1) | copy-start | bytes 28

commit v2 on v1

--- a/solution.py
+++ b/solution.py
@@ -218,12 +218,15 @@
     return total
 
 
-def cos_sin(turns, factor):
+def cos_sin_wide(turns, factor):
     magic = float(1.5 * 2.0**23)
     rest = turns - ((turns + magic) - magic)
     square = rest * rest
-    cosine = horner(square, COS_COEF * factor)
-    sine = horner(square, SIN_COEF * -factor) * rest
+    return horner(square, COS_COEF * factor), horner(square, SIN_COEF * -factor) * rest
+
+
+def cos_sin(turns, factor):
+    cosine, sine = cos_sin_wide(turns, factor)
     return cosine.astype(BF), sine.astype(BF)
 
 
@@ -236,62 +239,68 @@
     return jnp.dot(first, second, preferred_element_type=F32)
 
 
-def grid_tables(slabs, depths):
+def index_like(shape, axis):
+    return lax.broadcasted_iota(jnp.int32, shape, axis)
+
+
+def keep_halves(refs, rows, lanes, values):
+    refs[0][rows, lanes], refs[1][rows, lanes] = split(values)
+
+
+def build_tables(slabs, depths, forth, back, y_forth, y_back):
     grid_x, grid_z = CX * slabs, CZ * depths
-    rows = np.arange(grid_x * grid_z)
-    device, local = rows // (CX * CZ), rows % (CX * CZ)
-    at_x = device // depths * CX + local // CZ
-    at_z = device % depths * CZ + local % CZ
-    freq_x, freq_z = rows // grid_z, rows % grid_z
-    angles = (
-        -2.0 * np.pi * (freq_x[:, None] * at_x[None] / grid_x + freq_z[:, None] * at_z[None] / grid_z)
-    )
-    wide = np.block([[np.cos(angles), -np.sin(angles)], [np.sin(angles), np.cos(angles)]])
-    lines = np.arange(NY)
-    turn = -2.0 * np.pi * (lines[:, None] * lines[None] % NY) / NY
-    ahead = np.concatenate([np.cos(turn), np.sin(turn)], 1)
-
-    def halves(table):
-        table = table.astype(np.float32)
-        high = table.astype(jnp.bfloat16)
-        low = (table - high.astype(np.float32)).astype(jnp.bfloat16)
-        return high, low
-
-    wide_high, wide_low = halves(wide)
-    forth = np.concatenate([wide_high, wide_low, wide_high], 1)
-    back = np.concatenate([wide_high.T, wide_low.T, wide_high.T], 1)
-    y_high, y_low = halves(ahead)
-    y_forth = np.concatenate([y_high, y_low, y_high], 0)
-    y_back = np.concatenate([y_high.T, y_low.T, y_high.T], 0)
-    return forth, back, y_forth, y_back
-
-
-def triple_rows(values):
+    size = grid_x * grid_z
+    first, second = slice(0, size), slice(size, 2 * size)
+    for refs, freq_axis in ((forth, 0), (back, 1)):
+        freq = index_like((size, size), freq_axis)
+        cell = index_like((size, size), 1 - freq_axis)
+        device, local = cell // (CX * CZ), cell % (CX * CZ)
+        at_x = device // depths * CX + local // CZ
+        at_z = device % depths * CZ + local % CZ
+        turns = ((freq // grid_z * at_x) % grid_x).astype(F32) / grid_x
+        turns = turns + ((freq % grid_z * at_z) % grid_z).astype(F32) / grid_z
+        cosine, sine = cos_sin_wide(turns, 1.0)
+        keep_halves(refs, first, first, cosine)
+        keep_halves(refs, second, second, cosine)
+        keep_halves(refs, first, second, -sine if freq_axis == 0 else sine)
+        keep_halves(refs, second, first, sine if freq_axis == 0 else -sine)
+    line = (NY, NY)
+    turns = ((index_like(line, 0) * index_like(line, 1)) % NY).astype(F32) / NY
+    cosine, sine = cos_sin_wide(turns, 1.0)
+    first, second = slice(0, NY), slice(NY, 2 * NY)
+    keep_halves(y_forth, first, first, cosine)
+    keep_halves(y_forth, first, second, sine)
+    keep_halves(y_back, first, first, cosine)
+    keep_halves(y_back, second, first, sine)
+
+
+def times_table(table, values):
     high, low = split(values)
-    return jnp.concatenate([high, high, low], 0)
-
-
-def triple_lanes(values):
+    lanes = values.shape[1]
+    both = dot(table[0], jnp.concatenate([high, low], 1))
+    return both[:, :lanes] + both[:, lanes:] + dot(table[1], high)
+
+
+def table_times(values, table):
     high, low = split(values)
-    return jnp.concatenate([high, high, low], 1)
-
-
-def stage_forward(stack, count, forth, y_forth):
-    lines = dot(triple_lanes(stack), y_forth[...])
-    size = stack.shape[0] // count
-    pieces = [
-        jnp.concatenate([lines[i * size : (i + 1) * size, :NY], lines[i * size : (i + 1) * size, NY:]], 0)
-        for i in range(count)
-    ]
-    wide = pieces[0] if count == 1 else jnp.concatenate(pieces, 1)
-    out = dot(forth[...], triple_rows(wide))
+    return dot(high, table[0]) + dot(low, table[0]) + dot(high, table[1])
+
+
+def loaded(refs, rows=slice(None)):
+    return tuple(ref[rows] for ref in refs)
+
+
+def stage_forward(grid, forth, y_forth):
+    lines = table_times(grid, loaded(y_forth))
+    size = grid.shape[0]
+    out = times_table(loaded(forth), jnp.concatenate([lines[:, :NY], lines[:, NY:]], 0))
     return out[:size], out[size:]
 
 
-def stage_inverse(real_part, imag_part, back, y_back):
-    size = real_part.shape[0]
-    out = dot(back[...], triple_rows(jnp.concatenate([real_part, imag_part], 0)))
-    return dot(triple_lanes(jnp.concatenate([out[:size], out[size:]], 1)), y_back[...])
+def stage_inverse(real_part, imag_part, table, y_back):
+    out = times_table(table, jnp.concatenate([real_part, imag_part], 0))
+    size = out.shape[0] // 2
+    return table_times(jnp.concatenate([out[:size], out[size:]], 1), loaded(y_back))
 
 
 def full_sum(values):
@@ -299,7 +308,7 @@
 
 
 def transfer_of(psf, grid_z, forth, y_forth):
-    spec_re, spec_im = stage_forward(psf, 1, forth, y_forth)
+    spec_re, spec_im = stage_forward(psf, forth, y_forth)
     shape = psf.shape
     row = lax.broadcasted_iota(jnp.int32, shape, 0)
     lane = lax.broadcasted_iota(jnp.int32, shape, 1)
@@ -308,10 +317,10 @@
     return spec_re * scale, spec_im * scale
 
 
-def deconvolve(transfer, beam, forth, back, y_forth, y_back):
+def deconvolve(transfer, beam, forth, back, y_forth, y_back, whole, own_rows):
     total = float(beam.shape[0] * NY)
     trans_re, trans_im = transfer
-    beam_re, beam_im = stage_forward(beam, 1, forth, y_forth)
+    beam_re, beam_im = stage_forward(beam, forth, y_forth)
     power = trans_re * trans_re + trans_im * trans_im
     data_re = trans_re * beam_re + trans_im * beam_im
     data_im = trans_re * beam_im - trans_im * beam_re
@@ -320,14 +329,23 @@
         if sweep == 0:
             grad_re, grad_im = -data_re, -data_im
         else:
-            hat_re, hat_im = stage_forward(source, 1, forth, y_forth)
+            hat_re, hat_im = stage_forward(source, forth, y_forth)
             grad_re = power * hat_re - data_re
             grad_im = power * hat_im - data_im
         norm = grad_re * grad_re + grad_im * grad_im
         grad_norm = full_sum(norm) / total
         image_norm = full_sum(power * norm) / total
         step = grad_norm / (image_norm + 1e-06) / total
-        move = step * stage_inverse(grad_re, grad_im, back, y_back)
+        if sweep < ITERS - 1:
+            table = loaded(back)
+        else:
+            start, count = own_rows
+            size = beam.shape[0]
+            parts = [loaded(back, pl.ds(start + at, count)) for at in (0, size)]
+            table = [jnp.concatenate([parts[0][half], parts[1][half]], 0) for half in range(2)]
+            whole[...] = source
+            source = whole[pl.ds(start, count)]
+        move = step * stage_inverse(grad_re, grad_im, table, y_back)
         source = jnp.maximum(-move if sweep == 0 else source - move, 0.0)
     return source
 
@@ -396,17 +414,14 @@
     return spread
 
 
-def beam_chunk(chunk, spectra, store, bins):
-    mics = spectra.shape[2]
-    beam = jnp.zeros((1, 2 * NY), F32)
-    for which in range(bins):
-        steer_re = store[chunk, which, :mics]
-        steer_im = store[chunk, which, mics:]
-        first = dot(spectra[0, which], steer_re) + dot(spectra[1, which], steer_im)
-        second = dot(spectra[0, which], steer_im)
-        both = steer_re.astype(F32) * first + steer_im.astype(F32) * second
-        beam = beam + jnp.sum(both, axis=0, keepdims=True)
-    return beam
+def beam_chunk(chunk, which, spectra, store):
+    mics = spectra.shape[1]
+    steer_re = store[chunk, which, :mics]
+    steer_im = store[chunk, which, mics:]
+    first = dot(spectra[2 * which], steer_re) + dot(spectra[2 * which + 1], steer_im)
+    second = dot(spectra[2 * which], steer_im)
+    both = steer_re.astype(F32) * first + steer_im.astype(F32) * second
+    return jnp.sum(both, axis=0, keepdims=True)
 
 
 def put_chunk(ref, chunk, values):
@@ -428,16 +443,16 @@
 
 def whole_kernel(
     sizes,
+    csm_in,
+    positions_in,
+    order_in,
+    rates_in,
+    beam_ref,
+    source_ref,
     csm,
     positions,
     order,
     rates_ref,
-    forth_in,
-    back_in,
-    y_forth_in,
-    y_back_in,
-    beam_ref,
-    source_ref,
     spectra,
     store,
     near_x,
@@ -446,17 +461,24 @@
     mids,
     maps,
     own_psf,
-    forth,
-    back,
-    y_forth,
-    y_back,
-    result,
-    table_sem,
+    beam_more,
+    forth_high,
+    forth_low,
+    back_high,
+    back_low,
+    y_forth_high,
+    y_forth_low,
+    y_back_high,
+    y_back_low,
+    whole,
+    load_sem,
     block_sent,
     block_got,
     map_sent,
     map_got,
 ):
+    forth, back = (forth_high, forth_low), (back_high, back_low)
+    y_forth, y_back = (y_forth_high, y_forth_low), (y_back_high, y_back_low)
     size_x, size_y, size_z, bins = sizes
     grid_x, grid_z = CX * size_x, CZ * size_y * size_z
     mics = order.shape[1]
@@ -488,9 +510,9 @@
 
     lax.fori_loop(1, devices, greet, 0)
     loads = [
-        pltpu.make_async_copy(source, target, table_sem.at[i])
+        pltpu.make_async_copy(source, target, load_sem.at[i])
         for i, (source, target) in enumerate(
-            [(forth_in, forth), (back_in, back), (y_forth_in, y_forth), (y_back_in, y_back)]
+            [(csm_in, csm), (positions_in, positions), (order_in, order), (rates_in, rates_ref)]
         )
     ]
     for load in loads:
@@ -499,19 +521,23 @@
     def rows_of(block):
         return pl.ds(pl.multiple_of(block * share, share), share)
 
-    spectra[0, :, rows_of(own)] = csm[0]
-    spectra[1, :, rows_of(own)] = (csm[1].astype(F32) * -2.0).astype(BF)
+    pieces = 2 * bins
+    for load in loads:
+        load.wait()
+    for which in range(bins):
+        spectra[2 * which, rows_of(own)] = csm[0, which]
+        spectra[2 * which + 1, rows_of(own)] = (csm[1, which].astype(F32) * -2.0).astype(BF)
     pl.semaphore_wait(barrier, devices - 1)
 
     sends = []
 
-    def block_copy(block, way, target):
-        view = spectra.at[:, :, rows_of(block)]
+    def block_copy(piece, block, way, target):
+        view = spectra.at[piece, rows_of(block)]
         return pltpu.make_async_remote_copy(
             src_ref=view,
             dst_ref=view,
-            send_sem=block_sent.at[way, block],
-            recv_sem=block_got.at[block],
+            send_sem=block_sent.at[way, piece, block],
+            recv_sem=block_got.at[piece, block],
             device_id=target,
             device_id_type=MESH,
         )
@@ -521,76 +547,75 @@
     def along(sign):
         return {"gx": at_x + sign}
 
-    def send(valid, block, way, target):
-        sends.append((valid, block, way, target))
+    def send(valid, piece, block, way, target):
+        sends.append((valid, piece, block, way, target))
 
         @pl.when(valid)
         def _():
-            block_copy(block, way, target).start()
-
-    def await_block(valid, block):
+            block_copy(piece, block, way, target).start()
+
+    def await_block(valid, piece, block):
         @pl.when(valid)
         def _():
-            block_copy(block, SIBLING, sibling).wait_recv()
+            block_copy(piece, block, SIBLING, sibling).wait_recv()
 
     def inside(x):
         return (x >= 0) & (x < size_x)
 
     always = at_x >= 0
 
-    for sign, way in ((1, RIGHT), (-1, LEFT)):
-        send(inside(at_x + sign), own, way, along(sign))
-    send(always, own, ACROSS, across)
-    send(always, own, SIBLING, sibling)
-
-    def pass_on(distance):
+    def pass_on(piece, distance):
         for sign, way in ((1, RIGHT), (-1, LEFT)):
             source = at_x - sign * distance
             block = number(source, at_y, at_z)
             valid = inside(source)
-            await_block(valid, block)
+            if distance:
+                await_block(valid, piece, block)
             if distance < size_x - 1:
-                send(valid & inside(at_x + sign), block, way, along(sign))
-            send(valid, block, ACROSS, across)
-            send(valid, block, SIBLING, sibling)
-
-    def pass_across(distance):
+                send(valid & inside(at_x + sign), piece, block, way, along(sign))
+            if distance or sign == 1:
+                send(valid, piece, block, ACROSS, across)
+                send(valid, piece, block, SIBLING, sibling)
+
+    def pass_across(piece, distance):
         for sign in (1, -1) if distance else (1,):
             source = at_x - sign * distance
             block = number(source, 1 - at_y, at_z)
             valid = inside(source)
-            await_block(valid, block)
-            send(valid, block, SIBLING, sibling)
-
-    rates = [rates_ref[which] * (0.5 / math.pi) for which in range(bins)]
+            await_block(valid, piece, block)
+            send(valid, piece, block, SIBLING, sibling)
+
+    def exchange(slot):
+        for piece in range(pieces):
+            distance = slot - piece
+            if 0 <= distance < size_x:
+                pass_on(piece, distance)
+            if 0 <= distance - 2 < size_x:
+                pass_across(piece, distance - 2)
+
+    exchange(0)
+    rates = [rates_ref[0:1, which : which + 1] * (0.5 / math.pi) for which in range(bins)]
     prepare(
         order, positions, centre_of(grid_x, grid_z), rates, near_x, near_z, near_y, bins, factor, mids
     )
     near = (near_x, near_z, near_y)
     blocks = mics // 64
-
-    def steer(i, carry):
-        steer_rows(
-            i // blocks, i % blocks, depth_start, at_x, grid_x, grid_z, rates, near, store, bins, factor
-        )
-        return carry
-
     chunks = CX * CZ // 2
-    part = chunks * blocks // 4
-    for stage in range(4):
-        lax.fori_loop(part * stage, part * (stage + 1), steer, 0)
-        if stage < 3 and stage + 1 < size_x:
-            pass_on(stage + 1)
-        if 0 < stage < 3 and stage - 1 < size_x:
-            pass_across(stage - 1)
+    slots = max(chunks, pieces + size_x + 1)
+    for slot in range(1, slots):
+        if slot <= chunks:
+
+            def steer(i, carry):
+                steer_rows(
+                    i // blocks, i % blocks, depth_start, at_x, grid_x, grid_z, rates, near, store, bins, factor
+                )
+                return carry
+
+            lax.fori_loop(blocks * (slot - 1), blocks * slot, steer, 0)
+            put_chunk(own_psf, slot - 1, psf_chunk(slot - 1, mids, store, bins))
+        exchange(slot)
 
     rows = CX * CZ
-
-    def psf_step(chunk, carry):
-        put_chunk(own_psf, chunk, psf_chunk(chunk, mids, store, bins))
-        return carry
-
-    lax.fori_loop(0, chunks, psf_step, 0)
 
     def map_rows(device):
         return pl.ds(pl.multiple_of(device * rows, rows), rows)
@@ -623,32 +648,34 @@
         lax.fori_loop(1, devices, one, 0)
 
     spread_map(0, own_psf[...])
-    for distance in range(2, size_x):
-        pass_across(distance)
-    for x in range(size_x):
-        for y in range(size_y):
-            await_block(always, number(x, y, 1 - at_z))
-
-    def beam_step(chunk, carry):
-        put_chunk(beam_ref, chunk, beam_chunk(chunk, spectra, store, bins))
-        return carry
-
-    lax.fori_loop(0, chunks, beam_step, 0)
+    build_tables(size_x, size_y * size_z, forth, back, y_forth, y_back)
+    for which in range(bins):
+        for piece in (2 * which, 2 * which + 1):
+            for x in range(size_x):
+                for y in range(size_y):
+                    await_block(always, piece, number(x, y, 1 - at_z))
+
+        def beam_step(chunk, carry):
+            put_chunk(beam_ref if which == 0 else beam_more, chunk, beam_chunk(chunk, which, spectra, store))
+            return carry
+
+        lax.fori_loop(0, chunks, beam_step, 0)
+        if which:
+            beam_ref[...] = beam_ref[...] + beam_more[...]
     spread_map(1, beam_ref[...])
-    for load in loads:
-        load.wait()
     await_map(0)
     transfer = transfer_of(maps[0], grid_z, forth, y_forth)
     await_map(1)
-    result[...] = deconvolve(transfer, maps[1], forth, back, y_forth, y_back)
+    own_rows = (pl.multiple_of(own * rows, rows), rows)
+    source = deconvolve(transfer, maps[1], forth, back, y_forth, y_back, whole, own_rows)
     for x in range(CX):
-        source_ref[x] = result[pl.ds(pl.multiple_of(own * rows, rows) + x * CZ, CZ)]
-
-    for valid, block, way, target in sends:
+        source_ref[x] = source[x * CZ : (x + 1) * CZ]
+
+    for valid, piece, block, way, target in sends:
 
         @pl.when(valid)
         def _():
-            block_copy(block, way, target).wait_send()
+            block_copy(piece, block, way, target).wait_send()
 
     def sent(i, carry):
         for which in range(2):
@@ -663,30 +690,39 @@
     bins, mics = csm.shape[1], csm.shape[3]
     rows = CX * CZ
     devices = sizes[0] * sizes[1] * sizes[2]
+    size = devices * rows
     vmem = pl.BlockSpec(memory_space=pltpu.VMEM)
-    anywhere = pl.BlockSpec(memory_space=pl.ANY)
-    tables_of = [jnp.asarray(t) for t in grid_tables(sizes[0], sizes[1] * sizes[2])]
     beam, source = pl.pallas_call(
         functools.partial(whole_kernel, sizes),
         out_shape=[jax.ShapeDtypeStruct((CX, CZ, NY), F32)] * 2,
-        in_specs=[vmem, vmem, vmem, pl.BlockSpec(memory_space=pltpu.SMEM)] + [anywhere] * 4,
+        in_specs=[pl.BlockSpec(memory_space=pltpu.HBM)] * 4,
         out_specs=[vmem, vmem],
         scratch_shapes=[
-            pltpu.VMEM((2, bins, mics, mics), BF),
+            pltpu.VMEM(csm.shape, BF),
+            pltpu.VMEM(positions.shape, F32),
+            pltpu.VMEM((1, mics), jnp.int32),
+            pltpu.VMEM((1, bins), F32),
+            pltpu.VMEM((2 * bins, mics, mics), BF),
             pltpu.VMEM((rows // 2, bins, 2 * mics, 2 * NY), BF),
             pltpu.VMEM((mics, NY), F32),
             pltpu.VMEM((mics, NY), F32),
             pltpu.VMEM((mics, NY), F32),
             pltpu.VMEM((bins, 8, 2 * mics), BF),
-            pltpu.VMEM((2, devices * rows, NY), F32),
+            pltpu.VMEM((2, size, NY), F32),
             pltpu.VMEM((CX, CZ, NY), F32),
-        ]
-        + [pltpu.VMEM(t.shape, BF) for t in tables_of]
-        + [
-            pltpu.VMEM((devices * rows, NY), F32),
+            pltpu.VMEM((CX, CZ, NY), F32),
+            pltpu.VMEM((2 * size, 2 * size), BF),
+            pltpu.VMEM((2 * size, 2 * size), BF),
+            pltpu.VMEM((2 * size, 2 * size), BF),
+            pltpu.VMEM((2 * size, 2 * size), BF),
+            pltpu.VMEM((NY, 2 * NY), BF),
+            pltpu.VMEM((NY, 2 * NY), BF),
+            pltpu.VMEM((2 * NY, NY), BF),
+            pltpu.VMEM((2 * NY, NY), BF),
+            pltpu.VMEM((size, NY), F32),
             pltpu.SemaphoreType.DMA((4,)),
-            pltpu.SemaphoreType.DMA((4, devices)),
-            pltpu.SemaphoreType.DMA((devices,)),
+            pltpu.SemaphoreType.DMA((4, 2 * bins, devices)),
+            pltpu.SemaphoreType.DMA((2 * bins, devices)),
             pltpu.SemaphoreType.DMA((2, devices)),
             pltpu.SemaphoreType.DMA((2, devices)),
         ],
@@ -694,7 +730,7 @@
             vmem_limit_bytes=48 * 1024 * 1024, collective_id=0, has_side_effects=True
         ),
         name="maps_and_sources",
-    )(csm, positions, mic_order[None], wavenumbers, *tables_of)
+    )(csm, positions, mic_order[None], wavenumbers[None])
     return beam, source
 
 

time: 55.5 us -> 54.3 us (0.978)
  local copies, waits for them, and re-layouts: 8.8 us -> 3.47 us
  Pallas kernels: 45.7 us -> 50 us
    unnamed x18 -> x10, local copies, waits for them, and re-layouts: 8.8 us -> 3.47 us
    pallas_call x1, Pallas kernels: 45.7 us -> 50 us  [small_device(): pl.pallas_call(functools.partial(whole_kernel, sizes), out_shape=[jax.Sha...]
where the time goes in v2:
time: 54.3 us; the launch traced here: 54.1 us
  Pallas kernels  50 us (92%)
  local copies, waits for them, and re-layouts  3.47 us (6%)
  between operations  0.66 us (1%)
    pallas_call x1, Pallas kernels, small_device(): pl.pallas_call(functools.partial(whole_kernel, sizes), out_shape=[jax.Sha...  50 us
    unnamed x10, local copies, waits for them, and re-layouts  3.47 us

profile of v2, /device:TPU:0, one launch (start us, length us, event | category | flops | bytes accessed | tf_op | source)
XLA Modules:
  0.0 54.1 jit_solution(192479932297343413)
XLA Ops:
  0.6 0.0 copy-start.2
  0.6 0.0 copy-start.3
  0.7 0.7 %copy-done.2 = s32[512]{0:T(512)S(1)} copy-done((s32[512]{0:T(512)S(1)}, s32[512]{0:T(512)}, u32[]{:S(2)}) %copy-start.2) | copy-done | bytes 2072
  1.3 0.0 copy-done.3
  1.3 0.0 copy-start
  1.3 0.9 %copy-done = bf16[2,2,32,512]{3,2,1,0:T(8,128)(2,1)S(1)} copy-done((bf16[2,2,32,512]{3,2,1,0:T(8,128)(2,1)S(1)}, bf16[2,2,32,512]{3,2,1,0:T(8,128)(2,1)}, u32[]{:S(2)}) %copy-start) | copy-done | bytes 131096
  2.2 0.0 copy-start.1
  2.2 0.7 %copy-done.1 = f32[3,512]{1,0:T(4,128)S(1)} copy-done((f32[3,512]{1,0:T(4,128)S(1)}, f32[3,512]{1,0:T(4,128)}, u32[]{:S(2)}) %copy-start.1) | copy-done | bytes 6168
  2.9 50.0 %maps_and_sources.1 = (f32[4,4,128]{2,1,0:T(4,128)S(1)}, f32[4,4,128]{2,1,0:T(4,128)S(1)}) custom-call(bf16[2,2,32,512]{3,2,1,0:T(8,128)(2,1)S(1)} %copy-done, f32[3,512]{1,0:T(4,128)S(1)} %copy-done.1, s32[1,512]{1,0:T(1,128)S(1)} %bitcast.2, f32[1,2]{1,0:T(1,128)S(1)} %bitcast.3), custom_call_target="tpu_custom_call" | custom-call | tf_op jit(solution)/shard_map/maps_and_sources/pallas_call | solution.py:695
  52.9 0.6 %copy.8 = f32[4,4,128]{2,1,0:T(4,128)} copy(f32[4,4,128]{2,1,0:T(4,128)S(1)} %get-tuple-element.4) | data formatting | bytes 16384
  53.5 0.6 %copy.9 = f32[4,4,128]{2,1,0:T(4,128)} copy(f32[4,4,128]{2,1,0:T(4,128)S(1)} %get-tuple-element.5) | data formatting | bytes 16384
Async XLA Ops:
  0.6 0.7 %copy-start.2 = (s32[512]{0:T(512)S(1)}, s32[512]{0:T(512)}, u32[]{:S(2)}) copy-start(s32[512]{0:T(512)} %param.6) | copy-start | bytes 6148
  0.6 0.7 %copy-start.3 = (f32[2]{0:T(128)S(1)}, f32[2]{0:T(128)}, u32[]{:S(2)}) copy-start(f32[2]{0:T(128)} %param.7) | copy-start | bytes 28
  1.3 0.9 %copy-start = (bf16[2,2,32,512]{3,2,1,0:T(8,128)(2,1)S(1)}, bf16[2,2,32,512]{3,2,1,0:T(8,128)(2,1)}, u32[]{:S(2)}) copy-start(bf16[2,2,32,512]{3,2,1,0:T(8,128)(2,1)} %csm_in.1) | copy-start | bytes 393220
  2.2 0.7 %copy-start.1 = (f32[3,512]{1,0:T(4,128)S(1)}, f32[3,512]{1,0:T(4,128)}, u32[]{:S(2)}) copy-start(f32[3,512]{1,0:T(4,128)} %positions_in.1) | copy-start | bytes 18436

commit v3 on v2

--- a/solution.py
+++ b/solution.py
@@ -307,20 +307,25 @@
     return jnp.sum(jnp.sum(values, axis=0, keepdims=True), axis=1, keepdims=True)
 
 
-def transfer_of(psf, grid_z, forth, y_forth):
-    spec_re, spec_im = stage_forward(psf, forth, y_forth)
-    shape = psf.shape
-    row = lax.broadcasted_iota(jnp.int32, shape, 0)
-    lane = lax.broadcasted_iota(jnp.int32, shape, 1)
+def transfers_of(psf, beam, grid_z, forth, y_forth):
+    size = psf.shape[0]
+    lines = table_times(jnp.concatenate([psf, beam], 0), loaded(y_forth))
+    grids = [
+        jnp.concatenate([part[:, :NY], part[:, NY:]], 0) for part in (lines[:size], lines[size:])
+    ]
+    out = times_table(loaded(forth), jnp.concatenate(grids, 1))
+    row, lane = index_like(psf.shape, 0), index_like(psf.shape, 1)
     odd = (row // grid_z + row % grid_z + lane) % 2
     scale = (1.0 - 2.0 * odd.astype(F32)) / full_sum(psf)
-    return spec_re * scale, spec_im * scale
-
-
-def deconvolve(transfer, beam, forth, back, y_forth, y_back, whole, own_rows):
-    total = float(beam.shape[0] * NY)
+    transfer = (out[:size, :NY] * scale, out[size:, :NY] * scale)
+    return transfer, (out[:size, NY:], out[size:, NY:])
+
+
+def deconvolve(transfer, beam_hat, forth, back, y_forth, y_back, whole, own_rows):
     trans_re, trans_im = transfer
-    beam_re, beam_im = stage_forward(beam, forth, y_forth)
+    beam_re, beam_im = beam_hat
+    size = beam_re.shape[0]
+    total = float(size * NY)
     power = trans_re * trans_re + trans_im * trans_im
     data_re = trans_re * beam_re + trans_im * beam_im
     data_im = trans_re * beam_im - trans_im * beam_re
@@ -340,7 +345,6 @@
             table = loaded(back)
         else:
             start, count = own_rows
-            size = beam.shape[0]
             parts = [loaded(back, pl.ds(start + at, count)) for at in (0, size)]
             table = [jnp.concatenate([parts[0][half], parts[1][half]], 0) for half in range(2)]
             whole[...] = source
@@ -350,7 +354,7 @@
     return source
 
 
-def prepare(order, positions, centre, rates, near_x, near_z, near_y, bins, factor, mids):
+def prepare(order, positions, centre, rates, near_x, near_z, near_y, bins, factor, spectra):
     mics = order.shape[1]
     hot = (lax.broadcasted_iota(jnp.int32, (mics, mics), 0) == order[...]).astype(F32).astype(BF)
     values = jnp.concatenate([positions[...], jnp.zeros((5, mics), F32)], 0)
@@ -373,16 +377,8 @@
     dist = square * lax.rsqrt(square)
     for which in range(bins):
         cosine, sine = cos_sin(dist * rates[which], factor)
-        cosine, sine = cosine.astype(F32), sine.astype(F32)
-        rows = jnp.concatenate(
-            [
-                jnp.concatenate([cosine, sine], 1),
-                jnp.concatenate([sine, -cosine], 1),
-                jnp.zeros((6, 2 * mics), F32),
-            ],
-            0,
-        )
-        mids[which] = rows.astype(BF)
+        rows = [cosine.astype(F32), sine.astype(F32), jnp.zeros((14, mics), F32)]
+        spectra[2 * which, pl.ds(mics, 16)] = jnp.concatenate(rows, 0).astype(BF)
 
 
 def steer_rows(chunk, block, depth_start, slab, grid_x, grid_z, rates, near, store, bins, factor):
@@ -406,22 +402,18 @@
             store[chunk, which, below, half * NY : (half + 1) * NY] = sine
 
 
-def psf_chunk(chunk, mids, store, bins):
-    spread = jnp.zeros((1, 2 * NY), F32)
-    for which in range(bins):
-        dots = dot(mids[which], store[chunk, which])
-        spread = spread + (dots[0:1] * dots[0:1] + dots[1:2] * dots[1:2]) / bins
-    return spread
-
-
-def beam_chunk(chunk, which, spectra, store):
-    mics = spectra.shape[1]
+def map_chunk(chunk, which, spectra, store, bins):
+    mics = spectra.shape[2]
     steer_re = store[chunk, which, :mics]
     steer_im = store[chunk, which, mics:]
-    first = dot(spectra[2 * which], steer_re) + dot(spectra[2 * which + 1], steer_im)
-    second = dot(spectra[2 * which], steer_im)
-    both = steer_re.astype(F32) * first + steer_im.astype(F32) * second
-    return jnp.sum(both, axis=0, keepdims=True)
+    by_re = dot(spectra[2 * which], steer_re)
+    by_im = dot(spectra[2 * which], steer_im)
+    first = by_re[:mics] + dot(spectra[2 * which + 1, :mics], steer_im)
+    both = steer_re.astype(F32) * first + steer_im.astype(F32) * by_im[:mics]
+    real_dot = by_re[mics : mics + 1] + by_im[mics + 1 : mics + 2]
+    imag_dot = by_re[mics + 1 : mics + 2] - by_im[mics : mics + 1]
+    spread = (real_dot * real_dot + imag_dot * imag_dot) / bins
+    return jnp.sum(both, axis=0, keepdims=True), spread
 
 
 def put_chunk(ref, chunk, values):
@@ -458,10 +450,8 @@
     near_x,
     near_z,
     near_y,
-    mids,
     maps,
-    own_psf,
-    beam_more,
+    parts,
     forth_high,
     forth_low,
     back_high,
@@ -564,20 +554,18 @@
 
     always = at_x >= 0
 
-    def pass_on(piece, distance):
+    def from_line(piece, distance):
         for sign, way in ((1, RIGHT), (-1, LEFT)):
             source = at_x - sign * distance
             block = number(source, at_y, at_z)
             valid = inside(source)
-            if distance:
-                await_block(valid, piece, block)
+            await_block(valid, piece, block)
             if distance < size_x - 1:
                 send(valid & inside(at_x + sign), piece, block, way, along(sign))
-            if distance or sign == 1:
-                send(valid, piece, block, ACROSS, across)
-                send(valid, piece, block, SIBLING, sibling)
-
-    def pass_across(piece, distance):
+            send(valid, piece, block, ACROSS, across)
+            send(valid, piece, block, SIBLING, sibling)
+
+    def from_across(piece, distance):
         for sign in (1, -1) if distance else (1,):
             source = at_x - sign * distance
             block = number(source, 1 - at_y, at_z)
@@ -585,89 +573,94 @@
             await_block(valid, piece, block)
             send(valid, piece, block, SIBLING, sibling)
 
-    def exchange(slot):
-        for piece in range(pieces):
-            distance = slot - piece
-            if 0 <= distance < size_x:
-                pass_on(piece, distance)
-            if 0 <= distance - 2 < size_x:
-                pass_across(piece, distance - 2)
-
-    exchange(0)
+    events = []
+    for piece in range(pieces):
+        for distance in range(size_x):
+            if distance:
+                events.append((1.65 * distance + 0.65 * piece, from_line, piece, distance))
+            events.append((1.65 + 2.6 * distance + 0.65 * piece, from_across, piece, distance))
+    events.sort(key=lambda event: event[0])
+
+    for piece in range(pieces):
+        for sign, way in ((1, RIGHT), (-1, LEFT)):
+            send(inside(at_x + sign), piece, own, way, along(sign))
+        send(always, piece, own, ACROSS, across)
+        send(always, piece, own, SIBLING, sibling)
     rates = [rates_ref[0:1, which : which + 1] * (0.5 / math.pi) for which in range(bins)]
     prepare(
-        order, positions, centre_of(grid_x, grid_z), rates, near_x, near_z, near_y, bins, factor, mids
+        order, positions, centre_of(grid_x, grid_z), rates, near_x, near_z, near_y, bins, factor, spectra
     )
     near = (near_x, near_z, near_y)
     blocks = mics // 64
     chunks = CX * CZ // 2
-    slots = max(chunks, pieces + size_x + 1)
-    for slot in range(1, slots):
-        if slot <= chunks:
-
-            def steer(i, carry):
-                steer_rows(
-                    i // blocks, i % blocks, depth_start, at_x, grid_x, grid_z, rates, near, store, bins, factor
-                )
-                return carry
-
-            lax.fori_loop(blocks * (slot - 1), blocks * slot, steer, 0)
-            put_chunk(own_psf, slot - 1, psf_chunk(slot - 1, mids, store, bins))
-        exchange(slot)
+    count = chunks * blocks
+    step = 4
+
+    def steer(i, carry):
+        steer_rows(
+            i // blocks, i % blocks, depth_start, at_x, grid_x, grid_z, rates, near, store, bins, factor
+        )
+        return carry
+
+    done = 0
+    for start in range(0, count, step):
+        lax.fori_loop(start, start + step, steer, 0)
+        while done < len(events) * (start + step) // (count + 3 * step):
+            events[done][1](*events[done][2:])
+            done += 1
+    build_tables(size_x, size_y * size_z, forth, back, y_forth, y_back)
+    for event in events[done:]:
+        event[1](*event[2:])
 
     rows = CX * CZ
 
-    def map_rows(device):
-        return pl.ds(pl.multiple_of(device * rows, rows), rows)
-
-    def map_copy(which, i, source):
-        target = (own + i) % devices
-        return pltpu.make_async_remote_copy(
-            src_ref=maps.at[which, map_rows(source)],
-            dst_ref=maps.at[which, map_rows(source)],
-            send_sem=map_sent.at[which, i],
-            recv_sem=map_got.at[which, source],
-            device_id=place(target),
-            device_id_type=MESH,
-        )
-
-    def spread_map(which, values):
-        maps[which, map_rows(own)] = jnp.concatenate([values[x] for x in range(CX)], 0)
-
-        def start(i, carry):
-            map_copy(which, i, own).start()
-            return carry
-
-        lax.fori_loop(1, devices, start, 0)
-
-    def await_map(which):
-        def one(i, carry):
-            map_copy(which, i, (own + i) % devices).wait_recv()
-            return carry
-
-        lax.fori_loop(1, devices, one, 0)
-
-    spread_map(0, own_psf[...])
-    build_tables(size_x, size_y * size_z, forth, back, y_forth, y_back)
     for which in range(bins):
         for piece in (2 * which, 2 * which + 1):
             for x in range(size_x):
                 for y in range(size_y):
                     await_block(always, piece, number(x, y, 1 - at_z))
 
-        def beam_step(chunk, carry):
-            put_chunk(beam_ref if which == 0 else beam_more, chunk, beam_chunk(chunk, which, spectra, store))
+        def map_step(chunk, carry):
+            beam, spread = map_chunk(chunk, which, spectra, store, bins)
+            put_chunk(parts.at[which, 0], chunk, beam)
+            put_chunk(parts.at[which, 1], chunk, spread)
             return carry
 
-        lax.fori_loop(0, chunks, beam_step, 0)
-        if which:
-            beam_ref[...] = beam_ref[...] + beam_more[...]
-    spread_map(1, beam_ref[...])
-    await_map(0)
-    transfer = transfer_of(maps[0], grid_z, forth, y_forth)
-    await_map(1)
+        lax.fori_loop(0, chunks, map_step, 0)
+    for kind in range(2):
+        total = parts[0, kind]
+        for which in range(1, bins):
+            total = total + parts[which, kind]
+        maps[own, kind] = jnp.concatenate([total[x] for x in range(CX)], 0).astype(BF)
+        if kind == 0:
+            beam_ref[...] = total
+
+    def map_copy(i, source):
+        return pltpu.make_async_remote_copy(
+            src_ref=maps.at[source],
+            dst_ref=maps.at[source],
+            send_sem=map_sent.at[i],
+            recv_sem=map_got.at[source],
+            device_id=place((own + i) % devices),
+            device_id_type=MESH,
+        )
+
+    def spread_map(i, carry):
+        map_copy(i, own).start()
+        return carry
+
+    def await_map(i, carry):
+        map_copy(i, (own + i) % devices).wait_recv()
+        return carry
+
+    lax.fori_loop(1, devices, spread_map, 0)
+    lax.fori_loop(1, devices, await_map, 0)
+    size = devices * rows
+    beam = maps[:, 0].reshape(size, NY).astype(F32)
+    psf = maps[:, 1].reshape(size, NY).astype(F32)
+    transfer, beam_hat = transfers_of(psf, beam, grid_z, forth, y_forth)
     own_rows = (pl.multiple_of(own * rows, rows), rows)
-    source = deconvolve(transfer, maps[1], forth, back, y_forth, y_back, whole, own_rows)
+    source = deconvolve(transfer, beam_hat, forth, back, y_forth, y_back, whole, own_rows)
     for x in range(CX):
         source_ref[x] = source[x * CZ : (x + 1) * CZ]
 
@@ -678,8 +671,7 @@
             block_copy(piece, block, way, target).wait_send()
 
     def sent(i, carry):
-        for which in range(2):
-            map_copy(which, i, own).wait_send()
+        map_copy(i, own).wait_send()
         return carry
 
     lax.fori_loop(1, devices, sent, 0)
@@ -702,15 +694,13 @@
             pltpu.VMEM(positions.shape, F32),
             pltpu.VMEM((1, mics), jnp.int32),
             pltpu.VMEM((1, bins), F32),
-            pltpu.VMEM((2 * bins, mics, mics), BF),
+            pltpu.VMEM((2 * bins, mics + 16, mics), BF),
             pltpu.VMEM((rows // 2, bins, 2 * mics, 2 * NY), BF),
             pltpu.VMEM((mics, NY), F32),
             pltpu.VMEM((mics, NY), F32),
             pltpu.VMEM((mics, NY), F32),
-            pltpu.VMEM((bins, 8, 2 * mics), BF),
-            pltpu.VMEM((2, size, NY), F32),
-            pltpu.VMEM((CX, CZ, NY), F32),
-            pltpu.VMEM((CX, CZ, NY), F32),
+            pltpu.VMEM((devices, 2, rows, NY), BF),
+            pltpu.VMEM((bins, 2, CX, CZ, NY), F32),
             pltpu.VMEM((2 * size, 2 * size), BF),
             pltpu.VMEM((2 * size, 2 * size), BF),
             pltpu.VMEM((2 * size, 2 * size), BF),
@@ -723,11 +713,11 @@
             pltpu.SemaphoreType.DMA((4,)),
             pltpu.SemaphoreType.DMA((4, 2 * bins, devices)),
             pltpu.SemaphoreType.DMA((2 * bins, devices)),
-            pltpu.SemaphoreType.DMA((2, devices)),
-            pltpu.SemaphoreType.DMA((2, devices)),
+            pltpu.SemaphoreType.DMA((devices,)),
+            pltpu.SemaphoreType.DMA((devices,)),
         ],
         compiler_params=pltpu.CompilerParams(
-            vmem_limit_bytes=48 * 1024 * 1024, collective_id=0, has_side_effects=True
+            vmem_limit_bytes=60 * 1024 * 1024, collective_id=0, has_side_effects=True
         ),
         name="maps_and_sources",
     )(csm, positions, mic_order[None], wavenumbers[None])

time: 54.3 us -> 48.4 us (0.89)
  Pallas kernels: 50 us -> 45.7 us
  local copies, waits for them, and re-layouts: 3.47 us -> 1.9 us
    pallas_call x1, Pallas kernels: 50 us -> 45.7 us  [small_device(): pl.pallas_call(functools.partial(whole_kernel, sizes), out_shape=[jax.Sha...]
    unnamed x10 -> x4, local copies, waits for them, and re-layouts: 3.47 us -> 1.9 us
where the time goes in v3:
time: 48.4 us; the launch traced here: 48.3 us
  Pallas kernels  45.7 us (94%)
  local copies, waits for them, and re-layouts  1.9 us (4%)
  between operations  0.65 us (1%)
    pallas_call x1, Pallas kernels, small_device(): pl.pallas_call(functools.partial(whole_kernel, sizes), out_shape=[jax.Sha...  45.7 us
    unnamed x4, local copies, waits for them, and re-layouts  1.9 us

profile of v3, /device:TPU:0, one launch (start us, length us, event | category | flops | bytes accessed | tf_op | source)
XLA Modules:
  0.0 48.3 jit_solution(16035320688050210152)
XLA Ops:
  0.6 45.7 %maps_and_sources.1 = (f32[4,4,128]{2,1,0:T(4,128)}, f32[4,4,128]{2,1,0:T(4,128)}) custom-call(bf16[2,2,32,512]{3,2,1,0:T(8,128)(2,1)} %csm_in.1, f32[3,512]{1,0:T(4,128)} %positions_in.1, s32[1,512]{1,0:T(1,128)} %bitcast.2, f32[1,2]{1,0:T(1,128)} %bitcast.3), custom_call_target="tpu_custom_call" | custom-call | tf_op jit(solution)/shard_map/maps_and_sources/pallas_call | solution.py:687
  46.4 0.0 copy-start
  46.4 1.3 %copy.8 = f32[4,4,128]{2,1,0:T(4,128)} copy(f32[4,4,128]{2,1,0:T(4,128)} %get-tuple-element.4) | data formatting | bytes 16384
  47.7 0.0 copy-done
  47.7 0.6 %copy.9 = f32[4,4,128]{2,1,0:T(4,128)} copy(f32[4,4,128]{2,1,0:T(4,128)S(1)} %copy-done) | data formatting | bytes 16384
Async XLA Ops:
  46.4 1.3 %copy-start = (f32[4,4,128]{2,1,0:T(4,128)S(1)}, f32[4,4,128]{2,1,0:T(4,128)}, u32[]{:S(2)}) copy-start(f32[4,4,128]{2,1,0:T(4,128)} %get-tuple-element.5) | copy-start | bytes 24580

commit v4 on v3

--- a/solution.py
+++ b/solution.py
@@ -291,9 +291,10 @@
 
 
 def stage_forward(grid, forth, y_forth):
-    lines = table_times(grid, loaded(y_forth))
+    lines = dot(grid.astype(BF), y_forth[0][...])
     size = grid.shape[0]
-    out = times_table(loaded(forth), jnp.concatenate([lines[:, :NY], lines[:, NY:]], 0))
+    wide = jnp.concatenate([lines[:, :NY], lines[:, NY:]], 0).astype(BF)
+    out = dot(forth[0][...], wide)
     return out[:size], out[size:]
 
 
@@ -307,18 +308,12 @@
     return jnp.sum(jnp.sum(values, axis=0, keepdims=True), axis=1, keepdims=True)
 
 
-def transfers_of(psf, beam, grid_z, forth, y_forth):
-    size = psf.shape[0]
-    lines = table_times(jnp.concatenate([psf, beam], 0), loaded(y_forth))
-    grids = [
-        jnp.concatenate([part[:, :NY], part[:, NY:]], 0) for part in (lines[:size], lines[size:])
-    ]
-    out = times_table(loaded(forth), jnp.concatenate(grids, 1))
+def transfer_of(psf, grid_z, forth, y_forth):
+    spec_re, spec_im = stage_forward(psf, forth, y_forth)
     row, lane = index_like(psf.shape, 0), index_like(psf.shape, 1)
     odd = (row // grid_z + row % grid_z + lane) % 2
     scale = (1.0 - 2.0 * odd.astype(F32)) / full_sum(psf)
-    transfer = (out[:size, :NY] * scale, out[size:, :NY] * scale)
-    return transfer, (out[:size, NY:], out[size:, NY:])
+    return spec_re * scale, spec_im * scale
 
 
 def deconvolve(transfer, beam_hat, forth, back, y_forth, y_back, whole, own_rows):
@@ -354,7 +349,7 @@
     return source
 
 
-def prepare(order, positions, centre, rates, near_x, near_z, near_y, bins, factor, spectra):
+def prepare(order, positions, centre, rates, near_x, near_z, near_y, bins, factor, mids):
     mics = order.shape[1]
     hot = (lax.broadcasted_iota(jnp.int32, (mics, mics), 0) == order[...]).astype(F32).astype(BF)
     values = jnp.concatenate([positions[...], jnp.zeros((5, mics), F32)], 0)
@@ -377,11 +372,13 @@
     dist = square * lax.rsqrt(square)
     for which in range(bins):
         cosine, sine = cos_sin(dist * rates[which], factor)
-        rows = [cosine.astype(F32), sine.astype(F32), jnp.zeros((14, mics), F32)]
-        spectra[2 * which, pl.ds(mics, 16)] = jnp.concatenate(rows, 0).astype(BF)
-
-
-def steer_rows(chunk, block, depth_start, slab, grid_x, grid_z, rates, near, store, bins, factor):
+        rows = jnp.concatenate([cosine.astype(F32), sine.astype(F32), jnp.zeros((6, mics), F32)], 0)
+        column = rows.T
+        for part in range(2):
+            mids[which, part] = jnp.broadcast_to(column[:, part : part + 1], wide)
+
+
+def steer_rows(chunk, block, depth_start, slab, grid_x, grid_z, rates, near, store, bins, factor, mids, dots):
     near_x, near_z, near_y = near
     mics = near_x.shape[0]
     size = 64
@@ -400,20 +397,32 @@
             cosine, sine = cos_sin(dist * rates[which], factor)
             store[chunk, which, rows, half * NY : (half + 1) * NY] = cosine
             store[chunk, which, below, half * NY : (half + 1) * NY] = sine
-
-
-def map_chunk(chunk, which, spectra, store, bins):
+            cosine, sine = cosine.astype(F32), sine.astype(F32)
+            mid_re, mid_im = mids[which, 0, rows], mids[which, 1, rows]
+            real_dot = cosine * mid_re + sine * mid_im
+            imag_dot = cosine * mid_im - sine * mid_re
+            for part, value in enumerate((real_dot, imag_dot)):
+                folded = jnp.sum(value.reshape(size // 8, 8, NY), axis=0)
+                dots[chunk, which, part, :, half * NY : (half + 1) * NY] += folded
+
+
+def beam_chunk(chunk, which, spectra, store):
     mics = spectra.shape[2]
     steer_re = store[chunk, which, :mics]
     steer_im = store[chunk, which, mics:]
-    by_re = dot(spectra[2 * which], steer_re)
-    by_im = dot(spectra[2 * which], steer_im)
-    first = by_re[:mics] + dot(spectra[2 * which + 1, :mics], steer_im)
-    both = steer_re.astype(F32) * first + steer_im.astype(F32) * by_im[:mics]
-    real_dot = by_re[mics : mics + 1] + by_im[mics + 1 : mics + 2]
-    imag_dot = by_re[mics + 1 : mics + 2] - by_im[mics : mics + 1]
-    spread = (real_dot * real_dot + imag_dot * imag_dot) / bins
-    return jnp.sum(both, axis=0, keepdims=True), spread
+    first = dot(spectra[2 * which], steer_re) + dot(spectra[2 * which + 1], steer_im)
+    second = dot(spectra[2 * which], steer_im)
+    both = steer_re.astype(F32) * first + steer_im.astype(F32) * second
+    return jnp.sum(both, axis=0, keepdims=True)
+
+
+def spread_chunk(chunk, dots, bins):
+    spread = jnp.zeros((1, 2 * NY), F32)
+    for which in range(bins):
+        for part in range(2):
+            value = jnp.sum(dots[chunk, which, part], axis=0, keepdims=True)
+            spread = spread + value * value / bins
+    return spread
 
 
 def put_chunk(ref, chunk, values):
@@ -450,7 +459,10 @@
     near_x,
     near_z,
     near_y,
+    mids,
+    dots,
     maps,
+    own_psf,
     parts,
     forth_high,
     forth_low,
@@ -573,22 +585,35 @@
             await_block(valid, piece, block)
             send(valid, piece, block, SIBLING, sibling)
 
-    events = []
-    for piece in range(pieces):
-        for distance in range(size_x):
-            if distance:
-                events.append((1.65 * distance + 0.65 * piece, from_line, piece, distance))
-            events.append((1.65 + 2.6 * distance + 0.65 * piece, from_across, piece, distance))
-    events.sort(key=lambda event: event[0])
-
-    for piece in range(pieces):
+    def send_own(piece):
         for sign, way in ((1, RIGHT), (-1, LEFT)):
             send(inside(at_x + sign), piece, own, way, along(sign))
         send(always, piece, own, ACROSS, across)
         send(always, piece, own, SIBLING, sibling)
+
+    events = []
+    for piece in range(pieces):
+        late = 5.2 * (piece // 2) + 0.65 * (piece % 2)
+        if piece >= 2:
+            events.append((late - 2.6, piece // 2, send_own, piece))
+        for distance in range(size_x):
+            if distance:
+                events.append((1.65 * distance + late, piece // 2, from_line, piece, distance))
+            events.append((1.65 * (distance + 1) + late, piece // 2, from_across, piece, distance))
+    events.sort(key=lambda event: event[0])
+    first = 1 + max(i for i, event in enumerate(events) if event[1] == 0)
+    events, later = events[:first], events[first:]
+
+    def run(some):
+        for event in some:
+            event[2](*event[3:])
+
+    for piece in range(2):
+        send_own(piece)
+    dots[...] = jnp.zeros_like(dots)
     rates = [rates_ref[0:1, which : which + 1] * (0.5 / math.pi) for which in range(bins)]
     prepare(
-        order, positions, centre_of(grid_x, grid_z), rates, near_x, near_z, near_y, bins, factor, spectra
+        order, positions, centre_of(grid_x, grid_z), rates, near_x, near_z, near_y, bins, factor, mids
     )
     near = (near_x, near_z, near_y)
     blocks = mics // 64
@@ -598,67 +623,74 @@
 
     def steer(i, carry):
         steer_rows(
-            i // blocks, i % blocks, depth_start, at_x, grid_x, grid_z, rates, near, store, bins, factor
+            i // blocks, i % blocks, depth_start, at_x, grid_x, grid_z, rates, near, store, bins, factor, mids, dots
         )
         return carry
 
     done = 0
     for start in range(0, count, step):
         lax.fori_loop(start, start + step, steer, 0)
-        while done < len(events) * (start + step) // (count + 3 * step):
-            events[done][1](*events[done][2:])
-            done += 1
+        upto = len(events) * (start + step) // (count + 3 * step)
+        run(events[done:upto])
+        done = upto
+    for chunk in range(chunks):
+        put_chunk(own_psf, chunk, spread_chunk(chunk, dots, bins))
+
+    rows = CX * CZ
+
+    def map_copy(kind, i, source):
+        return pltpu.make_async_remote_copy(
+            src_ref=maps.at[kind, source],
+            dst_ref=maps.at[kind, source],
+            send_sem=map_sent.at[kind, i],
+            recv_sem=map_got.at[kind, source],
+            device_id=place((own + i) % devices),
+            device_id_type=MESH,
+        )
+
+    def spread_map(kind, values):
+        maps[kind, own] = jnp.concatenate([values[x] for x in range(CX)], 0).astype(BF)
+
+        def one(i, carry):
+            map_copy(kind, i, own).start()
+            return carry
+
+        lax.fori_loop(1, devices, one, 0)
+
+    def await_map(kind):
+        def one(i, carry):
+            map_copy(kind, i, (own + i) % devices).wait_recv()
+            return carry
+
+        lax.fori_loop(1, devices, one, 0)
+        return maps[kind].reshape(devices * rows, NY)
+
+    spread_map(0, own_psf[...])
     build_tables(size_x, size_y * size_z, forth, back, y_forth, y_back)
-    for event in events[done:]:
-        event[1](*event[2:])
-
-    rows = CX * CZ
-
+    run(events[done:])
     for which in range(bins):
         for piece in (2 * which, 2 * which + 1):
             for x in range(size_x):
                 for y in range(size_y):
                     await_block(always, piece, number(x, y, 1 - at_z))
 
-        def map_step(chunk, carry):
-            beam, spread = map_chunk(chunk, which, spectra, store, bins)
-            put_chunk(parts.at[which, 0], chunk, beam)
-            put_chunk(parts.at[which, 1], chunk, spread)
+        def beam_step(chunk, carry):
+            put_chunk(parts.at[which], chunk, beam_chunk(chunk, which, spectra, store))
             return carry
 
-        lax.fori_loop(0, chunks, map_step, 0)
-    for kind in range(2):
-        total = parts[0, kind]
-        for which in range(1, bins):
-            total = total + parts[which, kind]
-        maps[own, kind] = jnp.concatenate([total[x] for x in range(CX)], 0).astype(BF)
-        if kind == 0:
-            beam_ref[...] = total
-
-    def map_copy(i, source):
-        return pltpu.make_async_remote_copy(
-            src_ref=maps.at[source],
-            dst_ref=maps.at[source],
-            send_sem=map_sent.at[i],
-            recv_sem=map_got.at[source],
-            device_id=place((own + i) % devices),
-            device_id_type=MESH,
-        )
-
-    def spread_map(i, carry):
-        map_copy(i, own).start()
-        return carry
-
-    def await_map(i, carry):
-        map_copy(i, (own + i) % devices).wait_recv()
-        return carry
-
-    lax.fori_loop(1, devices, spread_map, 0)
-    lax.fori_loop(1, devices, await_map, 0)
-    size = devices * rows
-    beam = maps[:, 0].reshape(size, NY).astype(F32)
-    psf = maps[:, 1].reshape(size, NY).astype(F32)
-    transfer, beam_hat = transfers_of(psf, beam, grid_z, forth, y_forth)
+        if which == 0:
+            for chunk in range(0, chunks, 2):
+                lax.fori_loop(chunk, chunk + 2, beam_step, 0)
+                run(later[len(later) * chunk // chunks : len(later) * (chunk + 2) // chunks])
+        else:
+            lax.fori_loop(0, chunks, beam_step, 0)
+    total = parts[0]
+    for which in range(1, bins):
+        total = total + parts[which]
+    beam_ref[...] = total
+    spread_map(1, total)
+    transfer = transfer_of(await_map(0).astype(F32), grid_z, forth, y_forth)
+    beam_hat = stage_forward(await_map(1), forth, y_forth)
     own_rows = (pl.multiple_of(own * rows, rows), rows)
     source = deconvolve(transfer, beam_hat, forth, back, y_forth, y_back, whole, own_rows)
     for x in range(CX):
@@ -671,7 +703,8 @@
             block_copy(piece, block, way, target).wait_send()
 
     def sent(i, carry):
-        map_copy(i, own).wait_send()
+        for kind in range(2):
+            map_copy(kind, i, own).wait_send()
         return carry
 
     lax.fori_loop(1, devices, sent, 0)
@@ -694,13 +727,16 @@
             pltpu.VMEM(positions.shape, F32),
             pltpu.VMEM((1, mics), jnp.int32),
             pltpu.VMEM((1, bins), F32),
-            pltpu.VMEM((2 * bins, mics + 16, mics), BF),
+            pltpu.VMEM((2 * bins, mics, mics), BF),
             pltpu.VMEM((rows // 2, bins, 2 * mics, 2 * NY), BF),
             pltpu.VMEM((mics, NY), F32),
             pltpu.VMEM((mics, NY), F32),
             pltpu.VMEM((mics, NY), F32),
-            pltpu.VMEM((devices, 2, rows, NY), BF),
-            pltpu.VMEM((bins, 2, CX, CZ, NY), F32),
+            pltpu.VMEM((bins, 2, mics, NY), F32),
+            pltpu.VMEM((rows // 2, bins, 2, 8, 2 * NY), F32),
+            pltpu.VMEM((2, devices, rows, NY), BF),
+            pltpu.VMEM((CX, CZ, NY), F32),
+            pltpu.VMEM((bins, CX, CZ, NY), F32),
             pltpu.VMEM((2 * size, 2 * size), BF),
             pltpu.VMEM((2 * size, 2 * size), BF),
             pltpu.VMEM((2 * size, 2 * size), BF),
@@ -713,8 +749,8 @@
             pltpu.SemaphoreType.DMA((4,)),
             pltpu.SemaphoreType.DMA((4, 2 * bins, devices)),
             pltpu.SemaphoreType.DMA((2 * bins, devices)),
-            pltpu.SemaphoreType.DMA((devices,)),
-            pltpu.SemaphoreType.DMA((devices,)),
+            pltpu.SemaphoreType.DMA((2, devices)),
+            pltpu.SemaphoreType.DMA((2, devices)),
         ],
         compiler_params=pltpu.CompilerParams(
             vmem_limit_bytes=60 * 1024 * 1024, collective_id=0, has_side_effects=True

time: 48.4 us -> 55.2 us (1.14)
  Pallas kernels: 45.7 us -> 52.4 us
    pallas_call x1, Pallas kernels: 45.7 us -> 52.4 us  [small_device(): pl.pallas_call(functools.partial(whole_kernel, sizes), out_shape=[jax.Sha...]
where the time goes in v4:
time: 55.2 us; the launch traced here: 55 us
  Pallas kernels  52.4 us (95%)
  local copies, waits for them, and re-layouts  1.9 us (3%)
  between operations  0.65 us (1%)
    pallas_call x1, Pallas kernels, small_device(): pl.pallas_call(functools.partial(whole_kernel, sizes), out_shape=[jax.Sha...  52.4 us
    unnamed x4, local copies, waits for them, and re-layouts  1.9 us

profile of v4, /device:TPU:0, one launch (start us, length us, event | category | flops | bytes accessed | tf_op | source)
XLA Modules:
  0.0 55.0 jit_solution(835787412821469479)
XLA Ops:
  0.6 52.4 %maps_and_sources.1 = (f32[4,4,128]{2,1,0:T(4,128)}, f32[4,4,128]{2,1,0:T(4,128)}) custom-call(bf16[2,2,32,512]{3,2,1,0:T(8,128)(2,1)} %csm_in.1, f32[3,512]{1,0:T(4,128)} %positions_in.1, s32[1,512]{1,0:T(1,128)} %bitcast.2, f32[1,2]{1,0:T(1,128)} %bitcast.3), custom_call_target="tpu_custom_call" | custom-call | tf_op jit(solution)/shard_map/maps_and_sources/pallas_call | solution.py:720
  53.1 0.0 copy-start
  53.1 1.3 %copy.8 = f32[4,4,128]{2,1,0:T(4,128)} copy(f32[4,4,128]{2,1,0:T(4,128)} %get-tuple-element.4) | data formatting | bytes 16384
  54.4 0.0 copy-done
  54.4 0.6 %copy.9 = f32[4,4,128]{2,1,0:T(4,128)} copy(f32[4,4,128]{2,1,0:T(4,128)S(1)} %copy-done) | data formatting | bytes 16384
Async XLA Ops:
  53.1 1.3 %copy-start = (f32[4,4,128]{2,1,0:T(4,128)S(1)}, f32[4,4,128]{2,1,0:T(4,128)}, u32[]{:S(2)}) copy-start(f32[4,4,128]{2,1,0:T(4,128)} %get-tuple-element.5) | copy-start | bytes 24580

commit v5 on v3

--- a/solution.py
+++ b/solution.py
@@ -202,8 +202,8 @@
 def fit_coeffs():
     theta = (np.cos(np.pi * (np.arange(4000) + 0.5) / 4000) + 1.0) * 0.5 * 0.25
     turns = np.sqrt(theta)
-    cos_fit = np.polynomial.chebyshev.Chebyshev.fit(theta, np.cos(2 * np.pi * turns), 5)
-    sin_fit = np.polynomial.chebyshev.Chebyshev.fit(theta, np.sin(2 * np.pi * turns) / turns, 4)
+    cos_fit = np.polynomial.chebyshev.Chebyshev.fit(theta, np.cos(np.pi * turns), 3)
+    sin_fit = np.polynomial.chebyshev.Chebyshev.fit(theta, np.sin(np.pi * turns) / turns, 3)
     to_power = lambda fit: fit.convert(kind=np.polynomial.Polynomial).coef
     return to_power(cos_fit), to_power(sin_fit)
 
@@ -222,7 +222,9 @@
     magic = float(1.5 * 2.0**23)
     rest = turns - ((turns + magic) - magic)
     square = rest * rest
-    return horner(square, COS_COEF * factor), horner(square, SIN_COEF * -factor) * rest
+    root = math.sqrt(2.0 * factor)
+    half_sine = horner(square, SIN_COEF * root) * rest
+    return factor - half_sine * half_sine, horner(square, COS_COEF * -root) * half_sine
 
 
 def cos_sin(turns, factor):
@@ -291,9 +293,10 @@
 
 
 def stage_forward(grid, forth, y_forth):
-    lines = table_times(grid, loaded(y_forth))
+    lines = dot(grid.astype(BF), y_forth[0][...])
     size = grid.shape[0]
-    out = times_table(loaded(forth), jnp.concatenate([lines[:, :NY], lines[:, NY:]], 0))
+    wide = jnp.concatenate([lines[:, :NY], lines[:, NY:]], 0).astype(BF)
+    out = dot(forth[0][...], wide)
     return out[:size], out[size:]
 
 
@@ -309,14 +312,14 @@
 
 def transfers_of(psf, beam, grid_z, forth, y_forth):
     size = psf.shape[0]
-    lines = table_times(jnp.concatenate([psf, beam], 0), loaded(y_forth))
+    lines = dot(jnp.concatenate([psf, beam], 0), y_forth[0][...])
     grids = [
         jnp.concatenate([part[:, :NY], part[:, NY:]], 0) for part in (lines[:size], lines[size:])
     ]
-    out = times_table(loaded(forth), jnp.concatenate(grids, 1))
+    out = dot(forth[0][...], jnp.concatenate(grids, 1).astype(BF))
     row, lane = index_like(psf.shape, 0), index_like(psf.shape, 1)
     odd = (row // grid_z + row % grid_z + lane) % 2
-    scale = (1.0 - 2.0 * odd.astype(F32)) / full_sum(psf)
+    scale = (1.0 - 2.0 * odd.astype(F32)) / full_sum(psf.astype(F32))
     transfer = (out[:size, :NY] * scale, out[size:, :NY] * scale)
     return transfer, (out[:size, NY:], out[size:, NY:])
 
@@ -384,7 +387,7 @@
 def steer_rows(chunk, block, depth_start, slab, grid_x, grid_z, rates, near, store, bins, factor):
     near_x, near_z, near_y = near
     mics = near_x.shape[0]
-    size = 64
+    size = 128
     rows = pl.ds(pl.multiple_of(block * size, size), size)
     below = pl.ds(pl.multiple_of(mics + block * size, size), size)
     x_value = (2.0 * (slab * CX + chunk // (CZ // 2)).astype(F32) + 1.0) / grid_x - 1.0
@@ -591,10 +594,10 @@
         order, positions, centre_of(grid_x, grid_z), rates, near_x, near_z, near_y, bins, factor, spectra
     )
     near = (near_x, near_z, near_y)
-    blocks = mics // 64
+    blocks = mics // 128
     chunks = CX * CZ // 2
     count = chunks * blocks
-    step = 4
+    step = 2
 
     def steer(i, carry):
         steer_rows(
@@ -656,8 +659,8 @@
     lax.fori_loop(1, devices, spread_map, 0)
     lax.fori_loop(1, devices, await_map, 0)
     size = devices * rows
-    beam = maps[:, 0].reshape(size, NY).astype(F32)
-    psf = maps[:, 1].reshape(size, NY).astype(F32)
+    beam = maps[:, 0].reshape(size, NY)
+    psf = maps[:, 1].reshape(size, NY)
     transfer, beam_hat = transfers_of(psf, beam, grid_z, forth, y_forth)
     own_rows = (pl.multiple_of(own * rows, rows), rows)
     source = deconvolve(transfer, beam_hat, forth, back, y_forth, y_back, whole, own_rows)

time: 48.4 us -> 45.9 us (0.948)
  Pallas kernels: 45.7 us -> 43.2 us
    pallas_call x1, Pallas kernels: 45.7 us -> 43.2 us  [small_device(): pl.pallas_call(functools.partial(whole_kernel, sizes), out_shape=[jax.Sha...]
where the time goes in v5:
time: 45.9 us; the launch traced here: 45.8 us
  Pallas kernels  43.2 us (94%)
  local copies, waits for them, and re-layouts  1.9 us (4%)
  between operations  0.65 us (1%)
    pallas_call x1, Pallas kernels, small_device(): pl.pallas_call(functools.partial(whole_kernel, sizes), out_shape=[jax.Sha...  43.2 us
    unnamed x4, local copies, waits for them, and re-layouts  1.9 us

profile of v5, /device:TPU:0, one launch (start us, length us, event | category | flops | bytes accessed | tf_op | source)
XLA Modules:
  0.0 45.8 jit_solution(702784068699912260)
XLA Ops:
  0.6 43.2 %maps_and_sources.1 = (f32[4,4,128]{2,1,0:T(4,128)}, f32[4,4,128]{2,1,0:T(4,128)}) custom-call(bf16[2,2,32,512]{3,2,1,0:T(8,128)(2,1)} %csm_in.1, f32[3,512]{1,0:T(4,128)} %positions_in.1, s32[1,512]{1,0:T(1,128)} %bitcast.2, f32[1,2]{1,0:T(1,128)} %bitcast.3), custom_call_target="tpu_custom_call" | custom-call | tf_op jit(solution)/shard_map/maps_and_sources/pallas_call | solution.py:690
  43.9 0.0 copy-start
  43.9 1.3 %copy.8 = f32[4,4,128]{2,1,0:T(4,128)} copy(f32[4,4,128]{2,1,0:T(4,128)} %get-tuple-element.4) | data formatting | bytes 16384
  45.2 0.0 copy-done
  45.2 0.6 %copy.9 = f32[4,4,128]{2,1,0:T(4,128)} copy(f32[4,4,128]{2,1,0:T(4,128)S(1)} %copy-done) | data formatting | bytes 16384
Async XLA Ops:
  43.9 1.3 %copy-start = (f32[4,4,128]{2,1,0:T(4,128)S(1)}, f32[4,4,128]{2,1,0:T(4,128)}, u32[]{:S(2)}) copy-start(f32[4,4,128]{2,1,0:T(4,128)} %get-tuple-element.5) | copy-start | bytes 24580
